TPU v7x, 128 devices: a whole 4x4x4 slice. The times are simulated.
128 devices in a mesh: gx: 4 (over y_lo, core), gy: 4 (over z), gz: 8 (over y_hi, x).
Axes of the slice: x: 4, y: 4 (y_hi: 2, y_lo: 2; y = y_hi * 2 + y_lo), z: 4, core: 2. Of those that a mesh axis runs over, the one named last changes fastest.
Arguments:
- right_sides: float32 [6, 128, 128, 1024], P(None, 'gx', 'gy', 'gz'), may hold values from -6 to 6
- permeability: float32 [128, 128, 1024], P('gx', 'gy', 'gz'), may hold values from 0.1 to 10
Outputs:
- basis_q: float32 [24, 128, 128, 1024], P(None, 'gx', 'gy', 'gz')
- factor_r: float32 [24, 24], replicated
All inputs are finite; a program needn't handle non-finite values.
Results may differ from a plain program's by a relative error of at most 0.00012.
Values sent between devices are 32-bit elements; how exact they have to be, the bound alone decides.
A program may use at most 128 MiB of HBM per device.

v0:
```python
import jax
import jax.numpy as jnp
from jax import lax
from jax.sharding import PartitionSpec as P


def extended(cells, sides, width):
    for axis, dim in sides:
        count = lax.axis_size(axis)
        ends = count - 1
        head = lax.slice_in_dim(cells, 0, width, axis=dim)
        tail = lax.slice_in_dim(cells, cells.shape[dim] - width, cells.shape[dim], axis=dim)
        cells = jnp.concatenate(
            [
                lax.ppermute(tail, axis, [(i, (i + 1) % count) for i in range(ends)]),
                cells,
                lax.ppermute(head, axis, [((i + 1) % count, i) for i in range(ends)]),
            ],
            axis=dim,
        )
    return cells


def face_weights(kappa_pad):
    center = kappa_pad[1:-1, 1:-1, 1:-1]
    others = [
        kappa_pad[2:, 1:-1, 1:-1],
        kappa_pad[:-2, 1:-1, 1:-1],
        kappa_pad[1:-1, 2:, 1:-1],
        kappa_pad[1:-1, :-2, 1:-1],
        kappa_pad[1:-1, 1:-1, 2:],
        kappa_pad[1:-1, 1:-1, :-2],
    ]
    face_list = []
    for neighbour in others:
        divisor = center + neighbour
        divisor = jnp.where(divisor > 0, divisor, 1.0)
        face_list.append(2.0 * center * neighbour / divisor)
    diagonal = face_list[0]
    for weight in face_list[1:]:
        diagonal = diagonal + weight
    diagonal = jnp.where(diagonal > 0, diagonal, 1.0)
    return (face_list, diagonal)


def stencil(field_pad, face_list, diagonal):
    slices = [
        field_pad[:, 2:, 1:-1, 1:-1],
        field_pad[:, :-2, 1:-1, 1:-1],
        field_pad[:, 1:-1, 2:, 1:-1],
        field_pad[:, 1:-1, :-2, 1:-1],
        field_pad[:, 1:-1, 1:-1, 2:],
        field_pad[:, 1:-1, 1:-1, :-2],
    ]
    accum = face_list[0] * slices[0]
    for weight, piece in zip(face_list[1:], slices[1:]):
        accum = accum + weight * piece
    return 2.5 * accum / diagonal


def lower_factor(matrix):
    order = matrix.shape[0]
    positions = jnp.arange(order)
    lower = jnp.zeros_like(matrix)
    for column in range(order):
        remain = matrix[:, column] - jnp.dot(lower, lower[column], precision=lax.Precision.HIGHEST)
        pivot = jnp.sqrt(remain[column])
        entries = jnp.where(
            positions > column, remain / pivot, jnp.where(positions == column, pivot, 0.0)
        )
        lower = lower + entries[:, None] * (positions[None, :] == column).astype(matrix.dtype)
    return lower


def lower_inverse(lower):
    order = lower.shape[0]
    positions = jnp.arange(order)
    inverse = jnp.zeros_like(lower)
    for row_index in range(order):
        unit_row = (positions == row_index).astype(lower.dtype)
        partial_row = unit_row - jnp.dot(lower[row_index], inverse, precision=lax.Precision.HIGHEST)
        new_row = partial_row / lower[row_index, row_index]
        inverse = inverse + unit_row[:, None] * new_row[None, :]
    return inverse


def on_device(right_sides, permeability):
    depth = 3
    powers = [right_sides]
    kappa_pad = extended(permeability, (("gx", 0), ("gy", 1), ("gz", 2)), 1)
    face_list, diagonal = face_weights(kappa_pad)
    field = right_sides
    for power_index in range(depth):
        padded = extended(field, (("gx", 1), ("gy", 2), ("gz", 3)), 1)
        field = stencil(padded, face_list, diagonal)
        powers.append(field)
    basis = jnp.concatenate(powers, 0)
    columns = basis.shape[0]
    flat = basis.reshape(columns, -1)
    cell_count = flat.shape[1] * lax.axis_size("gx") * lax.axis_size("gy") * lax.axis_size("gz")
    gram = jnp.dot(flat, flat.T, precision=lax.Precision.HIGHEST)
    total_gram = lax.psum(gram, ("gx", "gy", "gz"))
    factor_r = lower_factor(total_gram / cell_count).T
    inverse = lower_inverse(factor_r.T)
    solved = jnp.dot(inverse, flat, precision=lax.Precision.HIGHEST)
    return (solved.reshape(basis.shape), factor_r)


def solution(mesh):
    placed = (P(None, "gx", "gy", "gz"), P("gx", "gy", "gz"))
    return jax.shard_map(
        on_device,
        mesh=mesh,
        in_specs=placed,
        out_specs=(P(None, "gx", "gy", "gz"), P()),
        check_vma=False,
    )
```

profile of v0, /device:TPU:1, one launch (start us, length us, event | category | flops | bytes accessed | tf_op | source)
XLA Modules:
  0.0 477.7 jit_solution(12275474916651257987)
XLA Ops:
  1.4 4.6 collective-permute-start.2
  6.0 1.9 collective-permute-start
  8.0 4.7 copy.166
  12.6 2.1 copy-done.5
  15.4 3.8 collective-permute-start.3
  19.2 1.9 collective-permute-start.1
  23.5 1.3 collective-permute-start.4
  24.9 4.2 collective-permute-start.6
  30.1 1.3 fusion.264
  31.3 1.5 copy.150
  32.8 1.3 collective-permute-start.8
  34.1 1.5 copy.154
  35.6 4.0 collective-permute-start.10
  39.6 2.8 copy_dynamic-update-slice_fusion
  42.5 2.1 copy-done.6
  44.6 1.3 collective-permute-start.5
  45.9 4.3 collective-permute-start.7
  50.7 1.2 copy.151
  51.9 1.2 copy.155
  53.3 2.7 pad_maximum_fusion.1
  56.0 5.2 %fusion.259 = (f32[6,34,34,1]{3,0,2,1:T(8,128)}, f32[6,34,34,1]{3,0,2,1:T(8,128)}) fusion(f32[6,34,34,128]{3,0,2,1:T(8,128)S(1)} %pad_maximum_fusion.1), kind=kLoop, calls=%fused_computation.574 | loop fusion | bytes 110976 | tf_op jit(solution)/shard_map/slice | solution.py:11
  61.2 3.9 copy.152
  65.2 1.3 collective-permute-start.9
  66.5 3.9 copy.156
  70.4 4.8 collective-permute-start.11
  75.2 4.7 compare_select_fusion
  79.9 4.4 copy.153
  84.3 4.3 copy.157
  88.6 15.8 %fusion.31 = f32[6,32,32,128]{3,0,2,1:T(8,128)S(1)} fusion(f32[6,34,34,1]{3,0,2,1:T(8,128)} %copy.157, f32[6,34,1,128]{3,0,2,1:T(8,128)S(1)} %collective-permute-done.5, f32[6,34,32,128]{3,0,2,1:T(8,128)} %copy-done.6, f32[6,34,1,128]{3,0,2,1:T(8,128)S(1)} %collective-permute-done.7, f32[6,34,34,1]{3,0,2,1:T(8,128)} %copy.153, ...), kind=kLoop, calls=%fused_computation.73 | loop fusion | flops 18087936 | bytes 13764800 | tf_op jit(solution)/shard_map/div | solution.py:58
  104.5 3.2 collective-permute-start.12
  107.7 4.9 %collective-permute-start.13 = (f32[6,1,32,128]{3,0,2,1:T(8,128)S(1)}, f32[6,1,32,128]{3,0,2,1:T(8,128)S(1)}, u32[]{:S(2)}, u32[]{:S(2)}) collective-permute-start(f32[6,1,32,128]{3,0,2,1:T(8,128)S(1)} %get-tuple-element.59), channel_id=1, source_target_pairs={{0,32},{32,64},{64,96},{1,33},{33,65},{65,97},{2,34},{34,66},{66,9... | collective-permute-start | bytes 294920 | tf_op jit(solution)/shard_map/ppermute | solution.py:15
  114.5 1.3 collective-permute-start.14
  115.8 4.3 collective-permute-start.15
  120.7 1.4 collective-permute-done.15
  123.2 5.2 %fusion.258 = (f32[6,34,34,1]{3,0,2,1:T(8,128)}, f32[6,34,34,1]{3,0,2,1:T(8,128)}) fusion(f32[6,34,34,128]{3,0,2,1:T(8,128)S(1)} %pad_maximum_fusion.2), kind=kLoop, calls=%fused_computation.573 | loop fusion | bytes 110976 | tf_op jit(solution)/shard_map/slice | solution.py:11
  128.4 3.3 copy.158
  131.7 1.3 collective-permute-start.16
  133.0 3.9 copy.160
  136.9 4.8 %collective-permute-start.17 = (f32[6,34,34,1]{2,3,1,0:T(1,128)}, f32[6,34,34,1]{2,3,1,0:T(1,128)}, u32[]{:S(2)}, u32[]{:S(2)}) collective-permute-start(f32[6,34,34,1]{2,3,1,0:T(1,128)} %copy.160), channel_id=1, source_target_pairs={{0,1},{1,2},{2,3},{3,4},{4,5},{5,6},{6,7},{8,9},{9,10},{10,11},{11... | collective-permute-start | bytes 83240 | tf_op jit(solution)/shard_map/ppermute | solution.py:15
  142.3 4.4 copy.159
  146.7 4.3 copy.161
  151.0 18.5 %fusion.18 = f32[6,32,32,128]{3,0,2,1:T(8,128)S(1)} fusion(f32[6,34,34,1]{3,0,2,1:T(8,128)} %copy.161, f32[6,34,1,128]{3,0,2,1:T(8,128)} %copy-done.14, f32[6,34,1,128]{3,0,2,1:T(8,128)} %copy-done.16, f32[6,1,32,128]{3,0,2,1:T(8,128)S(1)} %collective-permute-done.12, f32[6,32,32,128]{3,0,2,1:T(8,128)} %copy-done.1, ...), kind=kLoop, calls=%fused_computation.42 | loop fusion | flops 24379392 | bytes 10422464 | tf_op jit(solution)/shard_map/div | solution.py:58
  169.5 1.9 collective-permute-start.18
  171.4 5.8 %collective-permute-start.19 = (f32[6,1,32,128]{3,0,2,1:T(8,128)S(1)}, f32[6,1,32,128]{3,0,2,1:T(8,128)S(1)}, u32[]{:S(2)}, u32[]{:S(2)}) collective-permute-start(f32[6,1,32,128]{3,0,2,1:T(8,128)S(1)} %get-tuple-element.57), channel_id=1, source_target_pairs={{0,32},{32,64},{64,96},{1,33},{33,65},{65,97},{2,34},{34,66},{66,9... | collective-permute-start | bytes 294920 | tf_op jit(solution)/shard_map/ppermute | solution.py:15
  179.2 1.3 collective-permute-start.20
  180.5 4.7 collective-permute-start.21
  185.8 1.4 collective-permute-done.21
  188.3 5.2 %fusion.257 = (f32[6,34,34,1]{3,0,2,1:T(8,128)}, f32[6,34,34,1]{3,0,2,1:T(8,128)}) fusion(f32[6,34,34,128]{3,0,2,1:T(8,128)S(1)} %pad_maximum_fusion.3), kind=kLoop, calls=%fused_computation.572 | loop fusion | bytes 110976 | tf_op jit(solution)/shard_map/slice | solution.py:11
  193.5 3.3 copy.162
  196.8 1.3 collective-permute-start.22
  198.1 3.3 copy.164
  201.4 4.8 %collective-permute-start.23 = (f32[6,34,34,1]{2,3,1,0:T(1,128)S(1)}, f32[6,34,34,1]{2,3,1,0:T(1,128)S(1)}, u32[]{:S(2)}, u32[]{:S(2)}) collective-permute-start(f32[6,34,34,1]{2,3,1,0:T(1,128)S(1)} %copy.164), channel_id=1, source_target_pairs={{0,1},{1,2},{2,3},{3,4},{4,5},{5,6},{6,7},{8,9},{9,10},{10,11},{11... | collective-permute-start | bytes 83240 | tf_op jit(solution)/shard_map/ppermute | solution.py:15
  206.8 3.6 copy.163
  210.4 3.5 copy.165
  213.9 19.3 %fusion.5 = f32[6,32,32,128]{3,0,2,1:T(8,128)} fusion(f32[6,34,34,1]{3,0,2,1:T(8,128)} %copy.165, f32[6,34,1,128]{3,0,2,1:T(8,128)} %copy-done.13, f32[6,34,1,128]{3,0,2,1:T(8,128)} %copy-done.15, f32[6,1,32,128]{3,0,2,1:T(8,128)} %copy-done.11, f32[6,32,32,128]{3,0,2,1:T(8,128)} %copy-done.3, f32[6,1,32,128]{3,0,2,1:T(8,128)} %copy-done.12, ...), kind=kLoop, calls=%fused_computation.11 | loop fusion | flops 24379392 | bytes 10422464 | tf_op jit(solution)/shard_map/div | solution.py:58
  233.2 6.2 %pad_maximum_fusion = f32[24,32,32,128]{3,0,2,1:T(8,128)S(1)} fusion(f32[6,32,32,128]{3,0,2,1:T(8,128)} %fusion.5, f32[6,32,32,128]{3,0,2,1:T(8,128)S(1)} %copy-done.4, f32[6,32,32,128]{3,0,2,1:T(8,128)S(1)} %copy-done.2, f32[6,32,32,128]{3,0,2,1:T(8,128)} %copy-done.5), kind=kLoop, calls=%fused_computation.1 | loop fusion | flops 9437184 | bytes 25165824 | tf_op jit(solution)/shard_map/concatenate | solution.py:97
  239.5 4.8 copy-done
  244.4 13.1 %convolution_bitcast_fusion = f32[24,24]{1,0:T(8,128)S(1)} fusion(f32[24,32,32,128]{3,0,2,1:T(8,128)S(1)} %pad_maximum_fusion), kind=kOutput, calls=%fused_computation.99 | convolution fusion | flops 905969664 | bytes 12585216 | tf_op jit(solution)/shard_map/dot_general | solution.py:101
  257.5 83.5 %psum.7 = f32[24,24]{1,0:T(8,128)S(1)} all-reduce(f32[24,24]{1,0:T(8,128)S(1)} %convolution_bitcast_fusion), channel_id=1, replica_groups=mesh['gx'=4,'gy'=4,'gz'=8] {'gx','gy','gz'}, use_global_device_ids=true, to_apply=%region_0.1 | all-reduce | flops 576 | bytes 4608 | tf_op jit(solution)/shard_map/psum | solution.py:102
  381.4 11.5 %copy.167 = f32[24,32,32,128]{3,2,1,0:T(8,128)} copy(f32[24,32,32,128]{3,0,2,1:T(8,128)} %copy-done) | data formatting | bytes 25165824 | tf_op jit(solution)/shard_map/concatenate | solution.py:97
  409.7 16.8 %copy.180 = f32[3,8,1024,128]{3,1,2,0:T(8,128)} copy(f32[3,8,1024,128]{3,2,1,0:T(8,128)} %bitcast.525) | data formatting | bytes 25165824
  426.5 11.3 %copy.175 = f32[3,8,1024,128]{3,2,1,0:T(8,128)} copy(f32[3,8,1024,128]{3,1,2,0:T(8,128)} %copy.180) | data formatting | bytes 25165824
  441.0 24.5 %fusion = f32[24,32,32,128]{3,0,2,1:T(8,128)} fusion(f32[32,32,128,24]{2,1,0,3:T(8,128)} %bitcast.526, f32[24,24]{1,0:T(8,128)S(1)} %multiply_add_fusion.5, f32[24]{0:T(128)S(1)} %fusion.112, f32[24]{0:T(128)S(1)} %copy-done.44, f32[24]{0:T(128)S(1)} %fusion.111, f32[24]{0:T(128)S(1)} %copy-done.43, f32[24]{0:T(128)S(1)} %fusion.110, f32[24]{0:T(128)S(1)} %copy-done.42, ...), kind=kOutput, calls=%fused_computation.2 | convolution fusion | flops 905974272 | bytes 25168896 | tf_op jit(solution)/shard_map/dot_general | solution.py:105
  465.5 11.8 %copy.169 = f32[24,32,32,128]{3,2,1,0:T(8,128)} copy(f32[24,32,32,128]{3,0,2,1:T(8,128)} %fusion) | data formatting | bytes 25165824
  (270 shorter events, 58.0 us)
Async XLA Ops:
  0.6 21.7 %copy-start.10 = (f32[32,32,128]{2,1,0:T(8,128)S(1)}, f32[32,32,128]{2,1,0:T(8,128)}, u32[]{:S(2)}) copy-start(f32[32,32,128]{2,1,0:T(8,128)} %param.3) | copy-start | bytes 1572868
  1.4 20.9 %collective-permute-start.2 = (f32[1,32,128]{2,1,0:T(8,128)S(1)}, f32[1,32,128]{2,1,0:T(8,128)S(1)}, u32[]{:S(2)}, u32[]{:S(2)}) collective-permute-start(f32[1,32,128]{2,1,0:T(8,128)S(1)} %get-tuple-element.68), channel_id=1, source_target_pairs={{0,32},{32,64},{64,96},{1,33},{33,65},{65,97},{2,34},{34,66},{66,9... | collective-permute-start | bytes 49160 | tf_op jit(solution)/shard_map/ppermute | solution.py:15
  6.0 16.3 %collective-permute-start = (f32[1,32,128]{2,1,0:T(8,128)S(1)}, f32[1,32,128]{2,1,0:T(8,128)S(1)}, u32[]{:S(2)}, u32[]{:S(2)}) collective-permute-start(f32[1,32,128]{2,1,0:T(8,128)S(1)} %get-tuple-element.67), channel_id=1, source_target_pairs={{32,0},{64,32},{96,64},{33,1},{65,33},{97,65},{34,2},{66,34},{98,6... | collective-permute-start | bytes 49160 | tf_op jit(solution)/shard_map/ppermute | solution.py:17
  12.6 2.1 copy-start.5
  14.7 24.9 %copy-start.7 = (f32[6,32,32,128]{3,2,1,0:T(8,128)S(1)}, f32[6,32,32,128]{3,2,1,0:T(8,128)}, u32[]{:S(2)}) copy-start(f32[6,32,32,128]{3,2,1,0:T(8,128)} %param.2) | copy-start | bytes 9437188
  15.4 24.2 %collective-permute-start.3 = (f32[6,1,32,128]{3,0,2,1:T(8,128)}, f32[6,1,32,128]{3,0,2,1:T(8,128)S(1)}, u32[]{:S(2)}, u32[]{:S(2)}) collective-permute-start(f32[6,1,32,128]{3,0,2,1:T(8,128)} %get-tuple-element.62), channel_id=1, source_target_pairs={{0,32},{32,64},{64,96},{1,33},{33,65},{65,97},{2,34},{34,66},{66,9... | collective-permute-start | bytes 294920 | tf_op jit(solution)/shard_map/ppermute | solution.py:15
  19.2 23.2 %collective-permute-start.1 = (f32[6,1,32,128]{3,0,2,1:T(8,128)}, f32[6,1,32,128]{3,0,2,1:T(8,128)S(1)}, u32[]{:S(2)}, u32[]{:S(2)}) collective-permute-start(f32[6,1,32,128]{3,0,2,1:T(8,128)} %get-tuple-element.61), channel_id=1, source_target_pairs={{32,0},{64,32},{96,64},{33,1},{65,33},{97,65},{34,2},{66,34},{98,6... | collective-permute-start | bytes 294920 | tf_op jit(solution)/shard_map/ppermute | solution.py:17
  23.5 6.4 %copy-start.9 = (f32[34,32,128]{2,1,0:T(8,128)}, f32[34,32,128]{2,1,0:T(8,128)S(1)}, u32[]{:S(2)}) copy-start(f32[34,32,128]{2,1,0:T(8,128)S(1)} %constant_dynamic-update-slice_fusion) | copy-start | bytes 1671172
  23.5 6.1 %collective-permute-start.4 = (f32[34,1,128]{2,0,1:T(8,128)S(1)}, f32[34,1,128]{2,0,1:T(8,128)S(1)}, u32[]{:S(2)}, u32[]{:S(2)}) collective-permute-start(f32[34,1,128]{2,0,1:T(8,128)S(1)} %copy.172), channel_id=1, source_target_pairs={{8,0},{16,8},{24,16},{9,1},{17,9},{25,17},{10,2},{18,10},{26,18},{... | collective-permute-start | bytes 52232 | tf_op jit(solution)/shard_map/ppermute | solution.py:17
  24.9 5.1 %collective-permute-start.6 = (f32[34,1,128]{2,0,1:T(8,128)S(1)}, f32[34,1,128]{2,0,1:T(8,128)S(1)}, u32[]{:S(2)}, u32[]{:S(2)}) collective-permute-start(f32[34,1,128]{2,0,1:T(8,128)S(1)} %copy.173), channel_id=1, source_target_pairs={{0,8},{8,16},{16,24},{1,9},{9,17},{17,25},{2,10},{10,18},{18,26},{... | collective-permute-start | bytes 52232 | tf_op jit(solution)/shard_map/ppermute | solution.py:15
  29.7 12.7 %copy-start.24 = (f32[34,1,128]{2,1,0:T(1,128)}, f32[34,1,128]{2,1,0:T(1,128)S(1)}, u32[]{:S(2)}) copy-start(f32[34,1,128]{2,1,0:T(1,128)S(1)} %copy.144) | copy-start | bytes 52228
  30.0 12.4 %copy-start.26 = (f32[34,1,128]{2,1,0:T(1,128)}, f32[34,1,128]{2,1,0:T(1,128)S(1)}, u32[]{:S(2)}) copy-start(f32[34,1,128]{2,1,0:T(1,128)S(1)} %copy.147) | copy-start | bytes 52228
  32.8 17.9 %collective-permute-start.8 = (f32[34,34,1]{1,0,2:T(8,128)S(1)}, f32[34,34,1]{1,0,2:T(8,128)S(1)}, u32[]{:S(2)}, u32[]{:S(2)}) collective-permute-start(f32[34,34,1]{1,0,2:T(8,128)S(1)} %copy.150), channel_id=1, source_target_pairs={{1,0},{2,1},{3,2},{4,3},{5,4},{6,5},{7,6},{9,8},{10,9},{11,10},{12... | collective-permute-start | bytes 13880 | tf_op jit(solution)/shard_map/ppermute | solution.py:17
  35.6 16.4 %collective-permute-start.10 = (f32[34,34,1]{1,0,2:T(8,128)S(1)}, f32[34,34,1]{1,0,2:T(8,128)S(1)}, u32[]{:S(2)}, u32[]{:S(2)}) collective-permute-start(f32[34,34,1]{1,0,2:T(8,128)S(1)} %copy.154), channel_id=1, source_target_pairs={{0,1},{1,2},{2,3},{3,4},{4,5},{5,6},{6,7},{8,9},{9,10},{10,11},{11... | collective-permute-start | bytes 13880 | tf_op jit(solution)/shard_map/ppermute | solution.py:15
  39.6 5.0 %copy-start.17 = (f32[6,1,32,128]{3,0,2,1:T(8,128)}, f32[6,1,32,128]{3,0,2,1:T(8,128)S(1)}, u32[]{:S(2)}) copy-start(f32[6,1,32,128]{3,0,2,1:T(8,128)S(1)} %collective-permute-done.3) | copy-start | bytes 294916
  42.4 13.6 %copy-start.18 = (f32[6,1,32,128]{3,0,2,1:T(8,128)}, f32[6,1,32,128]{3,0,2,1:T(8,128)S(1)}, u32[]{:S(2)}) copy-start(f32[6,1,32,128]{3,0,2,1:T(8,128)S(1)} %collective-permute-done.1) | copy-start | bytes 294916
  42.4 2.1 copy-start.6
  44.6 8.6 %collective-permute-start.5 = (f32[6,34,1,128]{3,0,2,1:T(8,128)S(1)}, f32[6,34,1,128]{3,0,2,1:T(8,128)S(1)}, u32[]{:S(2)}, u32[]{:S(2)}) collective-permute-start(f32[6,34,1,128]{3,0,2,1:T(8,128)S(1)} %get-tuple-element.56), channel_id=1, source_target_pairs={{8,0},{16,8},{24,16},{9,1},{17,9},{25,17},{10,2},{18,10},{26,18},{... | collective-permute-start | bytes 313352 | tf_op jit(solution)/shard_map/ppermute | solution.py:17
  45.9 7.4 %collective-permute-start.7 = (f32[6,34,1,128]{3,0,2,1:T(8,128)S(1)}, f32[6,34,1,128]{3,0,2,1:T(8,128)S(1)}, u32[]{:S(2)}, u32[]{:S(2)}) collective-permute-start(f32[6,34,1,128]{3,0,2,1:T(8,128)S(1)} %get-tuple-element.55), channel_id=1, source_target_pairs={{0,8},{8,16},{16,24},{1,9},{9,17},{17,25},{2,10},{10,18},{18,26},{... | collective-permute-start | bytes 313352 | tf_op jit(solution)/shard_map/ppermute | solution.py:15
  61.2 13.9 %copy-start.25 = (f32[34,1,128]{2,1,0:T(1,128)S(1)}, f32[34,1,128]{2,1,0:T(1,128)}, u32[]{:S(2)}) copy-start(f32[34,1,128]{2,1,0:T(1,128)} %copy-done.24) | copy-start | bytes 52228
  61.2 13.9 %copy-start.27 = (f32[34,1,128]{2,1,0:T(1,128)S(1)}, f32[34,1,128]{2,1,0:T(1,128)}, u32[]{:S(2)}) copy-start(f32[34,1,128]{2,1,0:T(1,128)} %copy-done.26) | copy-start | bytes 52228
  61.2 13.9 %copy-start.34 = (f32[1,32,128]{2,1,0:T(8,128)S(1)}, f32[1,32,128]{2,1,0:T(8,128)}, u32[]{:S(2)}) copy-start(f32[1,32,128]{2,1,0:T(8,128)} %copy-done.33) | copy-start | bytes 49156
  61.2 13.9 %copy-start.36 = (f32[1,32,128]{2,1,0:T(8,128)S(1)}, f32[1,32,128]{2,1,0:T(8,128)}, u32[]{:S(2)}) copy-start(f32[1,32,128]{2,1,0:T(8,128)} %copy-done.35) | copy-start | bytes 49156
  65.2 14.7 %collective-permute-start.9 = (f32[6,34,34,1]{2,3,1,0:T(1,128)}, f32[6,34,34,1]{2,3,1,0:T(1,128)}, u32[]{:S(2)}, u32[]{:S(2)}) collective-permute-start(f32[6,34,34,1]{2,3,1,0:T(1,128)} %copy.152), channel_id=1, source_target_pairs={{1,0},{2,1},{3,2},{4,3},{5,4},{6,5},{7,6},{9,8},{10,9},{11,10},{12... | collective-permute-start | bytes 83240 | tf_op jit(solution)/shard_map/ppermute | solution.py:17
  70.4 13.9 %collective-permute-start.11 = (f32[6,34,34,1]{2,3,1,0:T(1,128)}, f32[6,34,34,1]{2,3,1,0:T(1,128)}, u32[]{:S(2)}, u32[]{:S(2)}) collective-permute-start(f32[6,34,34,1]{2,3,1,0:T(1,128)} %copy.156), channel_id=1, source_target_pairs={{0,1},{1,2},{2,3},{3,4},{4,5},{5,6},{6,7},{8,9},{9,10},{10,11},{11... | collective-permute-start | bytes 83240 | tf_op jit(solution)/shard_map/ppermute | solution.py:15
  79.9 71.1 %copy-start.8 = (f32[32,32,128]{2,1,0:T(8,128)}, f32[32,32,128]{2,1,0:T(8,128)S(1)}, u32[]{:S(2)}) copy-start(f32[32,32,128]{2,1,0:T(8,128)S(1)} %get-tuple-element.43) | copy-start | bytes 1572868
  104.4 17.7 %copy-start.1 = (f32[6,32,32,128]{3,0,2,1:T(8,128)}, f32[6,32,32,128]{3,0,2,1:T(8,128)S(1)}, u32[]{:S(2)}) copy-start(f32[6,32,32,128]{3,0,2,1:T(8,128)S(1)} %fusion.31) | copy-start | bytes 9437188
  104.5 8.8 %collective-permute-start.12 = (f32[6,1,32,128]{3,0,2,1:T(8,128)S(1)}, f32[6,1,32,128]{3,0,2,1:T(8,128)S(1)}, u32[]{:S(2)}, u32[]{:S(2)}) collective-permute-start(f32[6,1,32,128]{3,0,2,1:T(8,128)S(1)} %get-tuple-element.60), channel_id=1, source_target_pairs={{32,0},{64,32},{96,64},{33,1},{65,33},{97,65},{34,2},{66,34},{98,6... | collective-permute-start | bytes 294920 | tf_op jit(solution)/shard_map/ppermute | solution.py:17
  107.7 6.8 %collective-permute-start.13 = (f32[6,1,32,128]{3,0,2,1:T(8,128)S(1)}, f32[6,1,32,128]{3,0,2,1:T(8,128)S(1)}, u32[]{:S(2)}, u32[]{:S(2)}) collective-permute-start(f32[6,1,32,128]{3,0,2,1:T(8,128)S(1)} %get-tuple-element.59), channel_id=1, source_target_pairs={{0,32},{32,64},{64,96},{1,33},{33,65},{65,97},{2,34},{34,66},{66,9... | collective-permute-start | bytes 294920 | tf_op jit(solution)/shard_map/ppermute | solution.py:15
  114.5 6.1 %collective-permute-start.14 = (f32[6,34,1,128]{3,0,2,1:T(8,128)S(1)}, f32[6,34,1,128]{3,0,2,1:T(8,128)S(1)}, u32[]{:S(2)}, u32[]{:S(2)}) collective-permute-start(f32[6,34,1,128]{3,0,2,1:T(8,128)S(1)} %get-tuple-element.54), channel_id=1, source_target_pairs={{8,0},{16,8},{24,16},{9,1},{17,9},{25,17},{10,2},{18,10},{26,18},{... | collective-permute-start | bytes 313352 | tf_op jit(solution)/shard_map/ppermute | solution.py:17
  115.8 6.3 %collective-permute-start.15 = (f32[6,34,1,128]{3,0,2,1:T(8,128)S(1)}, f32[6,34,1,128]{3,0,2,1:T(8,128)S(1)}, u32[]{:S(2)}, u32[]{:S(2)}) collective-permute-start(f32[6,34,1,128]{3,0,2,1:T(8,128)S(1)} %get-tuple-element.53), channel_id=1, source_target_pairs={{0,8},{8,16},{16,24},{1,9},{9,17},{17,25},{2,10},{10,18},{18,26},{... | collective-permute-start | bytes 313352 | tf_op jit(solution)/shard_map/ppermute | solution.py:15
  120.7 1.5 copy-start.14
  131.7 10.6 %collective-permute-start.16 = (f32[6,34,34,1]{2,3,1,0:T(1,128)S(1)}, f32[6,34,34,1]{2,3,1,0:T(1,128)}, u32[]{:S(2)}, u32[]{:S(2)}) collective-permute-start(f32[6,34,34,1]{2,3,1,0:T(1,128)S(1)} %copy.158), channel_id=1, source_target_pairs={{1,0},{2,1},{3,2},{4,3},{5,4},{6,5},{7,6},{9,8},{10,9},{11,10},{12... | collective-permute-start | bytes 83240 | tf_op jit(solution)/shard_map/ppermute | solution.py:17
  136.9 9.7 %collective-permute-start.17 = (f32[6,34,34,1]{2,3,1,0:T(1,128)}, f32[6,34,34,1]{2,3,1,0:T(1,128)}, u32[]{:S(2)}, u32[]{:S(2)}) collective-permute-start(f32[6,34,34,1]{2,3,1,0:T(1,128)} %copy.160), channel_id=1, source_target_pairs={{0,1},{1,2},{2,3},{3,4},{4,5},{5,6},{6,7},{8,9},{9,10},{10,11},{11... | collective-permute-start | bytes 83240 | tf_op jit(solution)/shard_map/ppermute | solution.py:15
  169.5 17.7 %copy-start.3 = (f32[6,32,32,128]{3,0,2,1:T(8,128)}, f32[6,32,32,128]{3,0,2,1:T(8,128)S(1)}, u32[]{:S(2)}) copy-start(f32[6,32,32,128]{3,0,2,1:T(8,128)S(1)} %fusion.18) | copy-start | bytes 9437188
  169.5 8.4 %collective-permute-start.18 = (f32[6,1,32,128]{3,0,2,1:T(8,128)S(1)}, f32[6,1,32,128]{3,0,2,1:T(8,128)S(1)}, u32[]{:S(2)}, u32[]{:S(2)}) collective-permute-start(f32[6,1,32,128]{3,0,2,1:T(8,128)S(1)} %get-tuple-element.58), channel_id=1, source_target_pairs={{32,0},{64,32},{96,64},{33,1},{65,33},{97,65},{34,2},{66,34},{98,6... | collective-permute-start | bytes 294920 | tf_op jit(solution)/shard_map/ppermute | solution.py:17
  171.4 7.7 %collective-permute-start.19 = (f32[6,1,32,128]{3,0,2,1:T(8,128)S(1)}, f32[6,1,32,128]{3,0,2,1:T(8,128)S(1)}, u32[]{:S(2)}, u32[]{:S(2)}) collective-permute-start(f32[6,1,32,128]{3,0,2,1:T(8,128)S(1)} %get-tuple-element.57), channel_id=1, source_target_pairs={{0,32},{32,64},{64,96},{1,33},{33,65},{65,97},{2,34},{34,66},{66,9... | collective-permute-start | bytes 294920 | tf_op jit(solution)/shard_map/ppermute | solution.py:15
  177.9 9.3 %copy-start.11 = (f32[6,1,32,128]{3,0,2,1:T(8,128)}, f32[6,1,32,128]{3,0,2,1:T(8,128)S(1)}, u32[]{:S(2)}) copy-start(f32[6,1,32,128]{3,0,2,1:T(8,128)S(1)} %collective-permute-done.18) | copy-start | bytes 294916
  179.1 8.1 %copy-start.12 = (f32[6,1,32,128]{3,0,2,1:T(8,128)}, f32[6,1,32,128]{3,0,2,1:T(8,128)S(1)}, u32[]{:S(2)}) copy-start(f32[6,1,32,128]{3,0,2,1:T(8,128)S(1)} %collective-permute-done.19) | copy-start | bytes 294916
  179.2 6.6 %collective-permute-start.20 = (f32[6,34,1,128]{3,0,2,1:T(8,128)S(1)}, f32[6,34,1,128]{3,0,2,1:T(8,128)S(1)}, u32[]{:S(2)}, u32[]{:S(2)}) collective-permute-start(f32[6,34,1,128]{3,0,2,1:T(8,128)S(1)} %get-tuple-element.52), channel_id=1, source_target_pairs={{8,0},{16,8},{24,16},{9,1},{17,9},{25,17},{10,2},{18,10},{26,18},{... | collective-permute-start | bytes 313352 | tf_op jit(solution)/shard_map/ppermute | solution.py:17
  180.5 6.7 %collective-permute-start.21 = (f32[6,34,1,128]{3,0,2,1:T(8,128)S(1)}, f32[6,34,1,128]{3,0,2,1:T(8,128)S(1)}, u32[]{:S(2)}, u32[]{:S(2)}) collective-permute-start(f32[6,34,1,128]{3,0,2,1:T(8,128)S(1)} %get-tuple-element.51), channel_id=1, source_target_pairs={{0,8},{8,16},{16,24},{1,9},{9,17},{17,25},{2,10},{10,18},{18,26},{... | collective-permute-start | bytes 313352 | tf_op jit(solution)/shard_map/ppermute | solution.py:15
  196.8 10.0 %collective-permute-start.22 = (f32[6,34,34,1]{2,3,1,0:T(1,128)S(1)}, f32[6,34,34,1]{2,3,1,0:T(1,128)S(1)}, u32[]{:S(2)}, u32[]{:S(2)}) collective-permute-start(f32[6,34,34,1]{2,3,1,0:T(1,128)S(1)} %copy.162), channel_id=1, source_target_pairs={{1,0},{2,1},{3,2},{4,3},{5,4},{6,5},{7,6},{9,8},{10,9},{11,10},{12... | collective-permute-start | bytes 83240 | tf_op jit(solution)/shard_map/ppermute | solution.py:17
  201.4 9.0 %collective-permute-start.23 = (f32[6,34,34,1]{2,3,1,0:T(1,128)S(1)}, f32[6,34,34,1]{2,3,1,0:T(1,128)S(1)}, u32[]{:S(2)}, u32[]{:S(2)}) collective-permute-start(f32[6,34,34,1]{2,3,1,0:T(1,128)S(1)} %copy.164), channel_id=1, source_target_pairs={{0,1},{1,2},{2,3},{3,4},{4,5},{5,6},{6,7},{8,9},{9,10},{10,11},{11... | collective-permute-start | bytes 83240 | tf_op jit(solution)/shard_map/ppermute | solution.py:15
  213.9 19.3 %copy-start.2 = (f32[6,32,32,128]{3,0,2,1:T(8,128)S(1)}, f32[6,32,32,128]{3,0,2,1:T(8,128)}, u32[]{:S(2)}) copy-start(f32[6,32,32,128]{3,0,2,1:T(8,128)} %copy-done.1) | copy-start | bytes 9437188
  213.9 19.3 %copy-start.4 = (f32[6,32,32,128]{3,0,2,1:T(8,128)S(1)}, f32[6,32,32,128]{3,0,2,1:T(8,128)}, u32[]{:S(2)}) copy-start(f32[6,32,32,128]{3,0,2,1:T(8,128)} %copy-done.3) | copy-start | bytes 9437188
  239.5 4.8 %copy-start = (f32[24,32,32,128]{3,0,2,1:T(8,128)}, f32[24,32,32,128]{3,0,2,1:T(8,128)S(1)}, u32[]{:S(2)}) copy-start(f32[24,32,32,128]{3,0,2,1:T(8,128)S(1)} %pad_maximum_fusion) | copy-start | bytes 37748740
  244.2 107.1 %copy-start.19 = (f32[24]{0:T(128)S(1)}, f32[24]{0:T(128)}, u32[]{:S(2)}) copy-start(f32[24]{0:T(128)} %get-tuple-element.100) | copy-start | bytes 292
  244.2 108.7 %copy-start.20 = (f32[24]{0:T(128)S(1)}, f32[24]{0:T(128)}, u32[]{:S(2)}) copy-start(f32[24]{0:T(128)} %get-tuple-element.99) | copy-start | bytes 292
  244.2 110.2 %copy-start.21 = (f32[24]{0:T(128)S(1)}, f32[24]{0:T(128)}, u32[]{:S(2)}) copy-start(f32[24]{0:T(128)} %compare_convert_fusion.15) | copy-start | bytes 292
  244.3 111.8 %copy-start.22 = (f32[24]{0:T(128)S(1)}, f32[24]{0:T(128)}, u32[]{:S(2)}) copy-start(f32[24]{0:T(128)} %get-tuple-element.102) | copy-start | bytes 292
  244.3 113.4 %copy-start.23 = (f32[24]{0:T(128)S(1)}, f32[24]{0:T(128)}, u32[]{:S(2)}) copy-start(f32[24]{0:T(128)} %get-tuple-element.101) | copy-start | bytes 292
  244.3 115.0 %copy-start.28 = (f32[24]{0:T(128)S(1)}, f32[24]{0:T(128)}, u32[]{:S(2)}) copy-start(f32[24]{0:T(128)} %compare_convert_fusion.12) | copy-start | bytes 292
  244.3 116.6 %copy-start.29 = (f32[24]{0:T(128)S(1)}, f32[24]{0:T(128)}, u32[]{:S(2)}) copy-start(f32[24]{0:T(128)} %get-tuple-element.104) | copy-start | bytes 292
  244.3 118.2 %copy-start.30 = (f32[24]{0:T(128)S(1)}, f32[24]{0:T(128)}, u32[]{:S(2)}) copy-start(f32[24]{0:T(128)} %get-tuple-element.103) | copy-start | bytes 292
  244.3 119.8 %copy-start.31 = (f32[24]{0:T(128)S(1)}, f32[24]{0:T(128)}, u32[]{:S(2)}) copy-start(f32[24]{0:T(128)} %get-tuple-element.106) | copy-start | bytes 292
  244.3 121.5 %copy-start.32 = (f32[24]{0:T(128)S(1)}, f32[24]{0:T(128)}, u32[]{:S(2)}) copy-start(f32[24]{0:T(128)} %get-tuple-element.105) | copy-start | bytes 292
  244.3 123.1 %copy-start.37 = (f32[24]{0:T(128)S(1)}, f32[24]{0:T(128)}, u32[]{:S(2)}) copy-start(f32[24]{0:T(128)} %get-tuple-element.108) | copy-start | bytes 292
  244.3 124.8 %copy-start.38 = (f32[24]{0:T(128)S(1)}, f32[24]{0:T(128)}, u32[]{:S(2)}) copy-start(f32[24]{0:T(128)} %get-tuple-element.107) | copy-start | bytes 292
  244.3 126.5 %copy-start.39 = (f32[24]{0:T(128)S(1)}, f32[24]{0:T(128)}, u32[]{:S(2)}) copy-start(f32[24]{0:T(128)} %get-tuple-element.110) | copy-start | bytes 292
  244.3 128.2 %copy-start.40 = (f32[24]{0:T(128)S(1)}, f32[24]{0:T(128)}, u32[]{:S(2)}) copy-start(f32[24]{0:T(128)} %get-tuple-element.109) | copy-start | bytes 292
  244.4 129.8 %copy-start.41 = (f32[24]{0:T(128)S(1)}, f32[24]{0:T(128)}, u32[]{:S(2)}) copy-start(f32[24]{0:T(128)} %get-tuple-element.112) | copy-start | bytes 292
  244.4 131.4 %copy-start.42 = (f32[24]{0:T(128)S(1)}, f32[24]{0:T(128)}, u32[]{:S(2)}) copy-start(f32[24]{0:T(128)} %get-tuple-element.111) | copy-start | bytes 292
  244.4 133.0 %copy-start.43 = (f32[24]{0:T(128)S(1)}, f32[24]{0:T(128)}, u32[]{:S(2)}) copy-start(f32[24]{0:T(128)} %get-tuple-element.114) | copy-start | bytes 292
  244.4 134.7 %copy-start.44 = (f32[24]{0:T(128)S(1)}, f32[24]{0:T(128)}, u32[]{:S(2)}) copy-start(f32[24]{0:T(128)} %get-tuple-element.113) | copy-start | bytes 292
  (5 other events, 3.9 us)
where the time goes:
time: 487 us; the launch traced here: 478 us
  local copies, waits for them, and re-layouts  157 us (32%)
  blocking collectives  83.5 us (17%)
  other arithmetic  78 us (16%)
  starting transfers between devices  74.1 us (15%)
  matrix products  60.5 us (12%)
  between operations  18.3 us (4%)
  waiting for transfers between devices  6 us (1%)
    psum x1, blocking collectives, on_device(): total_gram = lax.psum(gram, ('gx', 'gy', 'gz'))  83.5 us
    unnamed x100, local copies, waits for them, and re-layouts  58.9 us
    ppermute x12, starting transfers between devices, extended(): lax.ppermute(tail, axis, [(i, (i + 1) % count) for i in range(ends)])  54.8 us
    div x3, other arithmetic, stencil(): return 2.5 * accum / diagonal  53.5 us
    slice x9, local copies, waits for them, and re-layouts, extended(): head = lax.slice_in_dim(cells, 0, width, axis=dim)  29.1 us
    dot_general x1, matrix products, on_device(): solved = jnp.dot(inverse, flat, precision=lax.Precision.HIGHEST)  24.5 us
    dot_general x24, matrix products, lower_inverse(): jnp.dot(lower[row_index], inverse, precision=lax.Precision.HIGHEST)  19.6 us
    ppermute x12, starting transfers between devices, extended(): lax.ppermute(head, axis, [((i + 1) % count, i) for i in range(ends)])  19.3 us
  transfers between devices with their start and end apart: 24, of which 8 were waited for; matrix products, arithmetic and copies ran while one was open for 10% of the time, Pallas kernels for 0%

commit v1 on v0

v1 whole, which is shorter than its diff:
```python
import functools

import jax
import jax.numpy as jnp
from jax import lax
from jax.experimental import pallas as pl
from jax.experimental.pallas import tpu as pltpu
from jax.sharding import PartitionSpec as P

NF = 6
DEPTH = 3
LEVELS = DEPTH + 1
NC = NF * LEVELS
CH = 8
TILES = 4
ROWS = NC * 8
MESH = pl.DeviceIdType.MESH
F32 = jnp.float32
BF16 = jnp.bfloat16
HIGH = lax.Precision.HIGHEST


def iota(shape, dim):
    return lax.broadcasted_iota(jnp.int32, shape, dim)


def nt(left, right, precision=None):
    return lax.dot_general(
        left, right, (((1,), (1,)), ((), ())), precision=precision, preferred_element_type=F32
    )


def lane_roll(value, amount):
    return pltpu.roll(value, amount % 128, 1)


def shifted_rows(tiles, before, after, row):
    rolled = [pltpu.roll(v, 1, 0) for v in tiles]
    upper = [jnp.where(row == 0, p, r) for p, r in zip([before] + rolled[:-1], rolled)]
    rolled = [pltpu.roll(v, 7, 0) for v in tiles]
    lower = [jnp.where(row == 7, n, r) for n, r in zip(rolled[1:] + [after], rolled)]
    return upper, lower


def shifted_lanes(value, pair, lane):
    left = lane_roll(jnp.where(lane == 127, pair, value), 1)
    right = lane_roll(jnp.where(lane == 0, pair, value), 127)
    return left, right


def basis_kernel(
    sizes, cells, rs, kap, hl, wmat, factor,
    kp, kys, kyr, kzs, kzr, vv, aa, ys, yr, zs, zr, acc, msg, slot1, slot2,
    load_sem, ks_sem, kr_sem, xs_sem, xr_sem, ys_sem, yr_sem, zs_sem, zr_sem,
    s1_sem, r1_sem, s2_sem, r2_sem,
):
    gx, gy, gz = sizes
    nx = kp.shape[0] - 2
    chunks = nx // CH
    ix, iy, iz = lax.axis_index("gx"), lax.axis_index("gy"), lax.axis_index("gz")
    at = {"gx": ix, "gy": iy, "gz": iz}
    size = {"gx": gx, "gy": gy, "gz": gz}

    def toward(axis, by):
        return {axis: lax.rem(at[axis] + (by + size[axis]), size[axis])}

    kap_copy = pltpu.make_async_copy(kap, kp.at[pl.ds(1, nx)], load_sem.at[NF])
    kap_copy.start()
    field_copies = []
    for f in range(NF):
        copy = pltpu.make_async_copy(rs.at[f], vv.at[0, pl.ds(1, nx), f], load_sem.at[f])
        copy.start()
        field_copies.append(copy)

    n1 = gx * gy
    rank1 = ix * gy + iy
    group1 = []
    for d in range(1, n1):
        other = lax.rem(rank1 + d, n1)
        group1.append({"gx": other // gy, "gy": lax.rem(other, gy)})
    group2 = [{"gz": lax.rem(iz + d, gz)} for d in range(1, gz)]
    barrier = pltpu.get_barrier_semaphore()
    for device in group1 + group2:
        pl.semaphore_signal(barrier, inc=1, device_id=device, device_id_type=MESH)

    lane = iota((8, 128), 1)
    row = iota((8, 128), 0)
    even = (lane & 1) == 0
    zero = jnp.zeros((8, 128), F32)

    def remote(src, dst, send, recv, device):
        return pltpu.make_async_remote_copy(
            src_ref=src, dst_ref=dst, send_sem=send, recv_sem=recv,
            device_id=device, device_id_type=MESH,
        )

    kap_copy.wait()

    def pack_kap(x, carry):
        tiles = [kp[x + 1, t * 8:(t + 1) * 8, :] for t in range(TILES)]
        kys[0, pl.ds(x, 1), :] = tiles[0][0:1]
        kys[1, pl.ds(x, 1), :] = tiles[3][7:8]
        result = []
        for m in range(2):
            both = jnp.where(lane < 64, lane_roll(tiles[2 * m], 1), lane_roll(tiles[2 * m + 1], 65))
            both = pltpu.roll(both, 2 * x, 1)
            result.append(jnp.where(((lane >> 1) & 31) == x, both, carry[m]))
        return tuple(result)

    packed = lax.fori_loop(0, nx, pack_kap, (zero, zero))
    for m in range(2):
        kzs[m] = packed[m]
    pl.semaphore_wait(barrier, n1 - 1 + gz - 1)

    kap_sends = [
        remote(kp.at[nx], kp.at[0], ks_sem.at[0], kr_sem.at[0], toward("gx", 1)),
        remote(kp.at[1], kp.at[nx + 1], ks_sem.at[1], kr_sem.at[1], toward("gx", -1)),
        remote(kys.at[1], kyr.at[0], ks_sem.at[2], kr_sem.at[2], toward("gy", 1)),
        remote(kys.at[0], kyr.at[1], ks_sem.at[3], kr_sem.at[3], toward("gy", -1)),
        remote(kzs, kzr.at[0], ks_sem.at[4], kr_sem.at[4], toward("gz", 1)),
        remote(kzs, kzr.at[1], ks_sem.at[5], kr_sem.at[5], toward("gz", -1)),
    ]
    for copy in kap_sends:
        copy.start()

    def x_copy(level, side):
        src, dst = (nx, 0) if side == 0 else (1, nx + 1)
        return remote(
            vv.at[level, src], vv.at[level, dst], xs_sem.at[level, side], xr_sem.at[level, side],
            toward("gx", 1 - 2 * side),
        )

    def y_copy(level, side, c):
        part = pl.ds(pl.multiple_of(c * CH, CH), CH)
        return remote(
            ys.at[level, 1 - side, :, part, :], yr.at[level, side, :, part, :],
            ys_sem.at[level, side, c], yr_sem.at[level, side, c], toward("gy", 1 - 2 * side),
        )

    def z_copy(level, side, c):
        return remote(
            zs.at[level, c], zr.at[level, side, c],
            zs_sem.at[level, side, c], zr_sem.at[level, side, c], toward("gz", 1 - 2 * side),
        )

    def emit(level, x, i, fields, carry):
        for f in range(0, NF, 2):
            at_row = (level * NF + f) * 8
            for t in range(TILES):
                full = jnp.concatenate([fields[f][t], fields[f + 1][t]], 0)
                high = full.astype(BF16)
                low = (full - high.astype(F32)).astype(BF16)
                hl[x, 0, at_row:at_row + 16, t * 128:(t + 1) * 128] = high
                hl[x, 1, at_row:at_row + 16, t * 128:(t + 1) * 128] = low
        if level == DEPTH:
            return carry
        result = []
        for m in range(NF // 2):
            merged = None
            for g in range(2 * TILES):
                piece = lane_roll(fields[2 * m + g // TILES][g % TILES], 16 * g + 1)
                merged = piece if merged is None else jnp.where(lane < 16 * g, merged, piece)
            merged = pltpu.roll(merged, 2 * i, 1)
            result.append(jnp.where(((lane >> 1) & 7) == i, merged, carry[m]))
        for f in range(NF):
            ys[level, 0, f, pl.ds(x, 1), :] = fields[f][0][0:1]
            ys[level, 1, f, pl.ds(x, 1), :] = fields[f][TILES - 1][7:8]
        return tuple(result)

    def send_chunk(level, q, c, carry):
        for m in range(NF // 2):
            zs[level, c, m] = carry[m]
        for side in range(2):
            y_copy(level, side, c).start()
            z_copy(level, side, c).start()
        if level > 0:
            @pl.when(q == 0)
            def _():
                x_copy(level, 1).start()

            @pl.when(q == 1)
            def _():
                x_copy(level, 0).start()

    def tiles_of(level, plane, f):
        return [vv[level, plane, f, t * 8:(t + 1) * 8, :] for t in range(TILES)]

    def order(q):
        return lax.rem(q * (chunks - 1), chunks)

    for copy in field_copies:
        copy.wait()
    for side in range(2):
        x_copy(0, side).start()

    def first_chunk(q, nothing):
        c = order(q)

        def plane(i, carry):
            x = c * CH + i
            return emit(0, x, i, [tiles_of(0, x + 1, f) for f in range(NF)], carry)

        send_chunk(0, q, c, lax.fori_loop(0, CH, plane, (zero,) * 3))
        return nothing

    lax.fori_loop(0, chunks, first_chunk, 0)

    for copy in kap_sends:
        copy.wait_recv()

    def inside(axis, by):
        edge = 0 if by < 0 else size[axis] - 1
        return jnp.where(at[axis] == edge, 0.0, 1.0).astype(F32)

    def weights(x, nothing):
        own = [kp[x + 1, t * 8:(t + 1) * 8, :] for t in range(TILES)]
        x_low = jnp.where(x == 0, inside("gx", -1), 1.0)
        x_high = jnp.where(x == nx - 1, inside("gx", 1), 1.0)
        before = jnp.broadcast_to(kyr[0, pl.ds(x, 1), :] * inside("gy", -1), (8, 128))
        after = jnp.broadcast_to(kyr[1, pl.ds(x, 1), :] * inside("gy", 1), (8, 128))
        upper, lower = shifted_rows(own, before, after, row)
        turned = []
        for m in range(2):
            both = jnp.where(even, kzr[0, m] * inside("gz", -1), kzr[1, m] * inside("gz", 1))
            turned.append(pltpu.roll(both, lax.rem(128 - 2 * x, 128), 1))
        for t in range(TILES):
            pair = lane_roll(turned[t // 2], 127 - 64 * (t % 2))
            left, right = shifted_lanes(own[t], pair, lane)
            part = slice(t * 8, (t + 1) * 8)
            others = [
                kp[x + 2, part, :] * x_high, kp[x, part, :] * x_low,
                lower[t], upper[t], right, left,
            ]
            faces = [2.0 * own[t] * other / (own[t] + other) for other in others]
            diagonal = faces[0]
            for face in faces[1:]:
                diagonal = diagonal + face
            scale = 2.5 / diagonal
            for n in range(6):
                aa[x, n, part, :] = faces[n] * scale
        return nothing

    lax.fori_loop(0, nx, weights, 0)

    for level in range(DEPTH):
        def chunk(q, nothing, level=level):
            c = order(q)
            for side in range(2):
                y_copy(level, side, c).wait_recv()
                z_copy(level, side, c).wait_recv()

            @pl.when(q == 0)
            def _():
                x_copy(level, 0).wait_recv()

            @pl.when(q == 1)
            def _():
                x_copy(level, 1).wait_recv()

            def plane(i, carry):
                x = c * CH + i
                turned = []
                for m in range(NF // 2):
                    both = jnp.where(even, zr[level, 0, c, m], zr[level, 1, c, m])
                    turned.append(pltpu.roll(both, lax.rem(128 - 2 * i, 128), 1))
                fields = []
                for f in range(NF):
                    own = tiles_of(level, x + 1, f)
                    low = tiles_of(level, x, f)
                    high = tiles_of(level, x + 2, f)
                    before = jnp.broadcast_to(yr[level, 0, f, pl.ds(x, 1), :], (8, 128))
                    after = jnp.broadcast_to(yr[level, 1, f, pl.ds(x, 1), :], (8, 128))
                    upper, lower = shifted_rows(own, before, after, row)
                    tiles = []
                    for t in range(TILES):
                        g = (f % 2) * TILES + t
                        pair = lane_roll(turned[f // 2], 127 - 16 * g)
                        left, right = shifted_lanes(own[t], pair, lane)
                        part = slice(t * 8, (t + 1) * 8)
                        total = aa[x, 0, part, :] * high[t]
                        total = total + aa[x, 1, part, :] * low[t]
                        total = total + aa[x, 2, part, :] * lower[t]
                        total = total + aa[x, 3, part, :] * upper[t]
                        total = total + aa[x, 4, part, :] * right
                        total = total + aa[x, 5, part, :] * left
                        tiles.append(total)
                        if level + 1 < DEPTH:
                            vv[level + 1, x + 1, f, part, :] = total
                    fields.append(tiles)
                return emit(level + 1, x, i, fields, carry)

            carry = lax.fori_loop(0, CH, plane, (zero,) * 3)
            if level + 1 < DEPTH:
                send_chunk(level + 1, q, c, carry)
            return nothing

        lax.fori_loop(0, chunks, chunk, 0)

    acc[...] = jnp.zeros_like(acc)

    def products(x, nothing):
        acc[...] += nt(hl[x].reshape(2 * ROWS, TILES * 128), hl[x, 0])
        return nothing

    lax.fori_loop(0, nx, products, 0)

    same = (iota((ROWS, ROWS), 0) & 7) == (iota((ROWS, ROWS), 1) & 7)
    mixed = jnp.where(same, acc[0:ROWS] + 2.0 * acc[ROWS:], 0.0)
    pick_rows = ((iota((NC, ROWS), 1) >> 3) == iota((NC, ROWS), 0)).astype(F32)
    spread = ((iota((ROWS, 128), 0) >> 3) == iota((ROWS, 128), 1)).astype(F32)
    small = jnp.dot(pick_rows, mixed, precision=HIGH, preferred_element_type=F32)
    small = jnp.dot(small, spread, precision=HIGH, preferred_element_type=F32)
    message = small[0:8] + lane_roll(small[8:16], 32) + lane_roll(small[16:24], 64)

    msg[0] = message
    slot1[rank1] = message
    sends1 = []
    for d, device in enumerate(group1):
        copy = remote(msg.at[0], slot1.at[rank1], s1_sem.at[d], r1_sem.at[rank1], device)
        copy.start()
        sends1.append(copy)
    for d in range(1, n1):
        source = lax.rem(rank1 + d, n1)
        remote(msg.at[0], slot1.at[source], s1_sem.at[0], r1_sem.at[source], group1[0]).wait_recv()
    message = slot1[0]
    for d in range(1, n1):
        message = message + slot1[d]
    msg[1] = message
    slot2[iz] = message
    sends2 = []
    for d, device in enumerate(group2):
        copy = remote(msg.at[1], slot2.at[iz], s2_sem.at[d], r2_sem.at[iz], device)
        copy.start()
        sends2.append(copy)
    for d in range(1, gz):
        source = lax.rem(iz + d, gz)
        remote(msg.at[1], slot2.at[source], s2_sem.at[0], r2_sem.at[source], group2[0]).wait_recv()
    message = slot2[0]
    for d in range(1, gz):
        message = message + slot2[d]

    message = message * (0.5 / cells)
    lanes = iota((NC, 128), 1)
    rows = iota((NC, 128), 0)
    parts = [message, lane_roll(message, 96), lane_roll(message, 64)]
    half = jnp.where(lanes < NC, jnp.concatenate(parts, 0), 0.0)
    identity = (lanes == rows).astype(F32)
    padded = jnp.concatenate([half, jnp.zeros((128 - NC, 128), F32)], 0)
    matrix = half + nt(identity, padded, HIGH) + (lanes == rows + 32).astype(F32)
    pivots = jnp.ones((NC, 128), F32)
    for k in range(NC):
        pivot_row = jnp.broadcast_to(matrix[k:k + 1, :], (NC, 128))
        column = jnp.broadcast_to(matrix[:, k:k + 1], (NC, 128))
        pivot = jnp.broadcast_to(column[k:k + 1, :], (NC, 128))
        pivots = jnp.where(rows == k, pivot, pivots)
        factors = jnp.where(rows > k, column / pivot, 0.0)
        matrix = matrix - factors * pivot_row
    matrix = matrix * (1.0 / jnp.sqrt(pivots))
    factor[...] = jnp.where((lanes >= rows) & (lanes < NC), matrix, 0.0)
    inverse = jnp.where(lanes <= rows, lane_roll(matrix, 96), 0.0)

    padded = jnp.concatenate([inverse, jnp.zeros((128 - NC, 128), F32)], 0)
    high = padded.astype(BF16)
    low = (padded - high.astype(F32)).astype(BF16)
    spread = spread.astype(BF16)
    for which, piece in enumerate((high, low)):
        wide = jnp.dot(spread, piece, preferred_element_type=F32).astype(BF16)
        wide = jnp.where(same, nt(wide, spread), 0.0).astype(BF16)
        wmat[which] = wide

    for copy in kap_sends + sends1 + sends2:
        copy.wait_send()
    for level in range(DEPTH):
        for side in range(2):
            x_copy(level, side).wait_send()

            def drain(c, nothing, level=level, side=side):
                y_copy(level, side, c).wait_send()
                z_copy(level, side, c).wait_send()
                return nothing

            lax.fori_loop(0, chunks, drain, 0)


def solve_kernel(wmat, factor, hl, q, r):
    x = pl.program_id(0)
    high, low = hl[x, 0], hl[x, 1]
    weights = jnp.concatenate([wmat[0], wmat[0], wmat[1]], 1)
    result = jnp.dot(weights, jnp.concatenate([high, low, high], 0), preferred_element_type=F32)
    for f in range(NC):
        for t in range(TILES):
            q[f, 0, t * 8:(t + 1) * 8, :] = result[f * 8:(f + 1) * 8, t * 128:(t + 1) * 128]

    @pl.when(x == 0)
    def _():
        r[...] = factor[:, 0:NC]


def on_device(sizes, right_sides, permeability):
    nx, ny, nz = permeability.shape
    chunks = nx // CH
    cells = float(nx * ny * nz * sizes[0] * sizes[1] * sizes[2])
    n1, n2 = sizes[0] * sizes[1], sizes[2]
    dma = pltpu.SemaphoreType.DMA
    vmem = pl.BlockSpec(memory_space=pltpu.VMEM)
    hl, wmat, factor = pl.pallas_call(
        functools.partial(basis_kernel, sizes, cells),
        out_shape=(
            pltpu.VMEM((nx, 2, ROWS, TILES * 128), BF16),
            pltpu.VMEM((2, ROWS, ROWS), BF16),
            pltpu.VMEM((NC, 128), F32),
        ),
        in_specs=[pl.BlockSpec(memory_space=pl.ANY)] * 2,
        out_specs=(vmem, vmem, vmem),
        scratch_shapes=[
            pltpu.VMEM((nx + 2, ny, 128), F32),
            pltpu.VMEM((2, nx, 128), F32),
            pltpu.VMEM((2, nx, 128), F32),
            pltpu.VMEM((2, 8, 128), F32),
            pltpu.VMEM((2, 2, 8, 128), F32),
            pltpu.VMEM((DEPTH, nx + 2, NF, ny, 128), F32),
            pltpu.VMEM((nx, 6, ny, 128), F32),
            pltpu.VMEM((DEPTH, 2, NF, nx, 128), F32),
            pltpu.VMEM((DEPTH, 2, NF, nx, 128), F32),
            pltpu.VMEM((DEPTH, chunks, NF // 2, 8, 128), F32),
            pltpu.VMEM((DEPTH, 2, chunks, NF // 2, 8, 128), F32),
            pltpu.VMEM((2 * ROWS, ROWS), F32),
            pltpu.VMEM((2, 8, 128), F32),
            pltpu.VMEM((n1, 8, 128), F32),
            pltpu.VMEM((n2, 8, 128), F32),
            dma((NF + 1,)),
            dma((6,)), dma((6,)),
            dma((DEPTH, 2)), dma((DEPTH, 2)),
            dma((DEPTH, 2, chunks)), dma((DEPTH, 2, chunks)),
            dma((DEPTH, 2, chunks)), dma((DEPTH, 2, chunks)),
            dma((n1 - 1,)), dma((n1,)),
            dma((n2 - 1,)), dma((n2,)),
        ],
        compiler_params=pltpu.CompilerParams(
            collective_id=0, has_side_effects=True, vmem_limit_bytes=44 * 1024 * 1024
        ),
        name="basis",
    )(right_sides, permeability)
    return pl.pallas_call(
        solve_kernel,
        grid=(nx,),
        out_shape=(
            jax.ShapeDtypeStruct((NC, nx, ny, 128), F32),
            jax.ShapeDtypeStruct((NC, NC), F32),
        ),
        in_specs=[vmem, vmem, vmem],
        out_specs=(
            pl.BlockSpec((NC, 1, ny, 128), lambda x: (0, x, 0, 0)),
            pl.BlockSpec((NC, NC), lambda x: (0, 0)),
        ),
        compiler_params=pltpu.CompilerParams(vmem_limit_bytes=8 * 1024 * 1024),
        name="solve",
    )(wmat, factor, hl)


def solution(mesh):
    sizes = tuple(mesh.shape[axis] for axis in ("gx", "gy", "gz"))
    return jax.shard_map(
        functools.partial(on_device, sizes),
        mesh=mesh,
        in_specs=(P(None, "gx", "gy", "gz"), P("gx", "gy", "gz")),
        out_specs=(P(None, "gx", "gy", "gz"), P()),
        check_vma=False,
    )
```

time: 487 us -> 100 us (0.21); the launches traced: 478 us -> 100 us
  local copies, waits for them, and re-layouts: 157 us -> 0 us
  Pallas kernels: 0 us -> 99.4 us
  blocking collectives: 83.5 us -> 0 us
  other arithmetic: 78 us -> 0 us
  starting transfers between devices: 74.1 us -> 0 us
  matrix products: 60.5 us -> 0 us
  between operations: 18.3 us -> 0.64 us
  waiting for transfers between devices: 6 us -> 0 us
    pallas_call x0 -> x2, Pallas kernels: none -> 99.4 us  [the longest x1 81.4 us: on_device(): pl.pallas_call(functools.partial(basis_kernel, sizes, cells), out_shape=(...]
    psum x1 -> x0, blocking collectives: 83.5 us -> none  [on_device(): total_gram = lax.psum(gram, ('gx', 'gy', 'gz'))]
    ppermute x24 -> x0, starting transfers between devices: 74.1 us -> none  [the longest x12 54.8 us: extended(): lax.ppermute(tail, axis, [(i, (i + 1) % count) for i in range(ends)])]
    dot_general x50 -> x0, matrix products: 60.5 us -> none  [the longest x1 24.5 us: on_device(): solved = jnp.dot(inverse, flat, precision=lax.Precision.HIGHEST)]
    slice x45 -> x0, local copies, waits for them, and re-layouts: 59.9 us -> none  [the longest x9 29.1 us: extended(): head = lax.slice_in_dim(cells, 0, width, axis=dim)]
    unnamed x100 -> x0, local copies, waits for them, and re-layouts: 58.9 us -> none
    div x4 -> x0, other arithmetic: 53.5 us -> none  [the longest x3 53.5 us: stencil(): return 2.5 * accum / diagonal]
    ppermute x10 -> x0, local copies, waits for them, and re-layouts: 27 us -> none  [the longest x5 13.6 us: extended(): lax.ppermute(head, axis, [((i + 1) % count, i) for i in range(ends)])]
  transfers between devices with their start and end apart: 24 -> 0, of which waited for: 8 -> 0; matrix products, arithmetic and copies ran while one was open for 10% -> 0% of each run, Pallas kernels for 0% -> 0%
where the time goes in v1:
time: 100 us
  Pallas kernels  99.4 us (99%)
    pallas_call x1, Pallas kernels, on_device(): pl.pallas_call(functools.partial(basis_kernel, sizes, cells), out_shape=(...  81.4 us
    pallas_call x1, Pallas kernels, on_device(): pl.pallas_call(solve_kernel, grid=(nx,), out_shape=(jax.ShapeDtypeStruct(...  18 us

profile of v1, /device:TPU:1, one launch (start us, length us, event | category | flops | bytes accessed | tf_op | source)
XLA Modules:
  0.0 100.0 jit_solution(6824187237052385298)
XLA Ops:
  0.6 81.4 %basis.1 = (bf16[32,2,192,512]{3,2,1,0:T(8,128)(2,1)S(1)}, bf16[2,192,192]{2,1,0:T(8,128)(2,1)S(1)}, f32[24,128]{1,0:T(8,128)S(1)}) custom-call(f32[6,32,32,128]{3,2,1,0:T(8,128)} %rs.1, f32[32,32,128]{2,1,0:T(8,128)} %kap.1), custom_call_target="tpu_custom_call" | custom-call | tf_op jit(solution)/shard_map/basis/pallas_call | solution.py:406
  82.0 18.0 %solve.1 = (f32[24,32,32,128]{3,2,1,0:T(8,128)}, f32[24,24]{1,0:T(8,128)}) custom-call(bf16[2,192,192]{2,1,0:T(8,128)(2,1)S(1)} %get-tuple-element.5.wmat, f32[24,128]{1,0:T(8,128)S(1)} %get-tuple-element.6.factor, bf16[32,2,192,512]{3,2,1,0:T(8,128)(2,1)S(1)} %get-tuple-element.7.hl), custom_call_target="tpu_custom_call" | custom-call | tf_op jit(solution)/shard_map/solve/pallas_call | solution.py:444

commit v2 on v1

--- a/solution.py
+++ b/solution.py
@@ -14,6 +14,11 @@
 CH = 8
 TILES = 4
 ROWS = NC * 8
+BAND = NF * 8
+UNIT = 4
+GROUP = 8
+SPAN = 4
+SLOTS = 4
 MESH = pl.DeviceIdType.MESH
 F32 = jnp.float32
 BF16 = jnp.bfloat16
@@ -28,6 +33,11 @@
     return lax.dot_general(
         left, right, (((1,), (1,)), ((), ())), precision=precision, preferred_element_type=F32
     )
+
+
+def reciprocal(value):
+    guess = pl.reciprocal(value, approx=True)
+    return guess * (2.0 - value * guess)
 
 
 def lane_roll(value, amount):
@@ -49,11 +59,13 @@
 
 
 def basis_kernel(
-    sizes, cells, rs, kap, hl, wmat, factor,
-    kp, kys, kyr, kzs, kzr, vv, aa, ys, yr, zs, zr, acc, msg, slot1, slot2,
+    sizes, cells, rs, kap, hl0, hl1, hl2, hl3, wmat, factor,
+    kp, kys, kyr, kzs, kzr, v0, v1, v2, aa, ys, yr, zs, zr, shift, gather, acc, msg, slot1, slot2,
     load_sem, ks_sem, kr_sem, xs_sem, xr_sem, ys_sem, yr_sem, zs_sem, zr_sem,
     s1_sem, r1_sem, s2_sem, r2_sem,
 ):
+    hl = (hl0, hl1, hl2, hl3)
+    vv = (v0, v1, v2)
     gx, gy, gz = sizes
     nx = kp.shape[0] - 2
     chunks = nx // CH
@@ -68,7 +80,7 @@
     kap_copy.start()
     field_copies = []
     for f in range(NF):
-        copy = pltpu.make_async_copy(rs.at[f], vv.at[0, pl.ds(1, nx), f], load_sem.at[f])
+        copy = pltpu.make_async_copy(rs.at[f], v0.at[pl.ds(1, nx), f], load_sem.at[f])
         copy.start()
         field_copies.append(copy)
 
@@ -94,6 +106,15 @@
             device_id=device, device_id_type=MESH,
         )
 
+    source, target = iota((256, 256), 0) & 127, iota((256, 256), 1)
+    wanted = jnp.where(target < 128, target - 1, target - 127)
+    shift[0:256] = (source == wanted).astype(F32).astype(BF16)
+    wanted = jnp.where((source & 1) == 0, 0, 255)
+    shift[256:512] = (target == wanted).astype(F32).astype(BF16)
+    source, target = iota((256, 128), 0) & 127, iota((256, 128), 1)
+    wanted = jnp.where((target & 1) == 0, 127, 0)
+    gather[...] = (source == wanted).astype(F32).astype(BF16)
+
     kap_copy.wait()
 
     def pack_kap(x, carry):
@@ -107,7 +128,7 @@
             result.append(jnp.where(((lane >> 1) & 31) == x, both, carry[m]))
         return tuple(result)
 
-    packed = lax.fori_loop(0, nx, pack_kap, (zero, zero))
+    packed = lax.fori_loop(0, nx, pack_kap, (zero, zero), unroll=8)
     for m in range(2):
         kzs[m] = packed[m]
     pl.semaphore_wait(barrier, n1 - 1 + gz - 1)
@@ -126,7 +147,7 @@
     def x_copy(level, side):
         src, dst = (nx, 0) if side == 0 else (1, nx + 1)
         return remote(
-            vv.at[level, src], vv.at[level, dst], xs_sem.at[level, side], xr_sem.at[level, side],
+            vv[level].at[src], vv[level].at[dst], xs_sem.at[level, side], xr_sem.at[level, side],
             toward("gx", 1 - 2 * side),
         )
 
@@ -143,36 +164,42 @@
             zs_sem.at[level, side, c], zr_sem.at[level, side, c], toward("gz", 1 - 2 * side),
         )
 
-    def emit(level, x, i, fields, carry):
+    def emit(level, x, fields):
         for f in range(0, NF, 2):
-            at_row = (level * NF + f) * 8
             for t in range(TILES):
                 full = jnp.concatenate([fields[f][t], fields[f + 1][t]], 0)
                 high = full.astype(BF16)
                 low = (full - high.astype(F32)).astype(BF16)
-                hl[x, 0, at_row:at_row + 16, t * 128:(t + 1) * 128] = high
-                hl[x, 1, at_row:at_row + 16, t * 128:(t + 1) * 128] = low
-        if level == DEPTH:
-            return carry
-        result = []
+                hl[level][x, 0, f * 8:f * 8 + 16, t * 128:(t + 1) * 128] = high
+                hl[level][x, 1, f * 8:f * 8 + 16, t * 128:(t + 1) * 128] = low
+        if level < DEPTH:
+            for f in range(NF):
+                ys[level, 0, f, pl.ds(x, 1), :] = fields[f][0][0:1]
+                ys[level, 1, f, pl.ds(x, 1), :] = fields[f][TILES - 1][7:8]
+
+    def halves(level, x, count, t):
+        part = slice(t * 128, (t + 1) * 128)
+        return jnp.concatenate(
+            [hl[level][pl.ds(x, count), h, :, part].reshape(count * BAND, 128) for h in range(2)], 1
+        )
+
+    def pack_chunk(level, c):
+        result = [zero] * (NF // 2)
+        for t in range(TILES):
+            outer = jnp.dot(
+                halves(level, c * CH, CH, t), gather[...], preferred_element_type=F32
+            )
+            for i in range(CH):
+                for f in range(NF):
+                    at_row = (i * NF + f) * 8
+                    mask = (lane >> 1) == ((f % 2) * TILES + t) * CH + i
+                    result[f // 2] = jnp.where(mask, outer[at_row:at_row + 8], result[f // 2])
         for m in range(NF // 2):
-            merged = None
-            for g in range(2 * TILES):
-                piece = lane_roll(fields[2 * m + g // TILES][g % TILES], 16 * g + 1)
-                merged = piece if merged is None else jnp.where(lane < 16 * g, merged, piece)
-            merged = pltpu.roll(merged, 2 * i, 1)
-            result.append(jnp.where(((lane >> 1) & 7) == i, merged, carry[m]))
-        for f in range(NF):
-            ys[level, 0, f, pl.ds(x, 1), :] = fields[f][0][0:1]
-            ys[level, 1, f, pl.ds(x, 1), :] = fields[f][TILES - 1][7:8]
-        return tuple(result)
-
-    def send_chunk(level, q, c, carry):
-        for m in range(NF // 2):
-            zs[level, c, m] = carry[m]
+            zs[level, c, m] = result[m]
+
+    def send_chunk(level, q, c):
         for side in range(2):
             y_copy(level, side, c).start()
-            z_copy(level, side, c).start()
         if level > 0:
             @pl.when(q == 0)
             def _():
@@ -182,8 +209,12 @@
             def _():
                 x_copy(level, 0).start()
 
+        pack_chunk(level, c)
+        for side in range(2):
+            z_copy(level, side, c).start()
+
     def tiles_of(level, plane, f):
-        return [vv[level, plane, f, t * 8:(t + 1) * 8, :] for t in range(TILES)]
+        return [vv[level][plane, f, t * 8:(t + 1) * 8, :] for t in range(TILES)]
 
     def order(q):
         return lax.rem(q * (chunks - 1), chunks)
@@ -196,11 +227,13 @@
     def first_chunk(q, nothing):
         c = order(q)
 
-        def plane(i, carry):
+        def plane(i, nothing):
             x = c * CH + i
-            return emit(0, x, i, [tiles_of(0, x + 1, f) for f in range(NF)], carry)
-
-        send_chunk(0, q, c, lax.fori_loop(0, CH, plane, (zero,) * 3))
+            emit(0, x, [tiles_of(0, x + 1, f) for f in range(NF)])
+            return nothing
+
+        lax.fori_loop(0, CH, plane, 0, unroll=2)
+        send_chunk(0, q, c)
         return nothing
 
     lax.fori_loop(0, chunks, first_chunk, 0)
@@ -231,16 +264,20 @@
                 kp[x + 2, part, :] * x_high, kp[x, part, :] * x_low,
                 lower[t], upper[t], right, left,
             ]
-            faces = [2.0 * own[t] * other / (own[t] + other) for other in others]
+            faces = [2.0 * own[t] * other * reciprocal(own[t] + other) for other in others]
             diagonal = faces[0]
             for face in faces[1:]:
                 diagonal = diagonal + face
-            scale = 2.5 / diagonal
+            scale = 2.5 * reciprocal(diagonal)
             for n in range(6):
                 aa[x, n, part, :] = faces[n] * scale
         return nothing
 
-    lax.fori_loop(0, nx, weights, 0)
+    lax.fori_loop(0, nx, weights, 0, unroll=2)
+
+    wide_lane = iota((16, 128), 1)
+    second = jnp.where(iota((16, 128), 0) < 8, 0, TILES)
+    groups = [((wide_lane >> 4) == second + t).astype(F32) for t in range(TILES)]
 
     for level in range(DEPTH):
         def chunk(q, nothing, level=level):
@@ -257,52 +294,83 @@
             def _():
                 x_copy(level, 1).wait_recv()
 
-            def plane(i, carry):
-                x = c * CH + i
-                turned = []
-                for m in range(NF // 2):
-                    both = jnp.where(even, zr[level, 0, c, m], zr[level, 1, c, m])
-                    turned.append(pltpu.roll(both, lax.rem(128 - 2 * i, 128), 1))
-                fields = []
-                for f in range(NF):
-                    own = tiles_of(level, x + 1, f)
-                    low = tiles_of(level, x, f)
-                    high = tiles_of(level, x + 2, f)
-                    before = jnp.broadcast_to(yr[level, 0, f, pl.ds(x, 1), :], (8, 128))
-                    after = jnp.broadcast_to(yr[level, 1, f, pl.ds(x, 1), :], (8, 128))
-                    upper, lower = shifted_rows(own, before, after, row)
-                    tiles = []
-                    for t in range(TILES):
-                        g = (f % 2) * TILES + t
-                        pair = lane_roll(turned[f // 2], 127 - 16 * g)
-                        left, right = shifted_lanes(own[t], pair, lane)
-                        part = slice(t * 8, (t + 1) * 8)
-                        total = aa[x, 0, part, :] * high[t]
-                        total = total + aa[x, 1, part, :] * low[t]
-                        total = total + aa[x, 2, part, :] * lower[t]
-                        total = total + aa[x, 3, part, :] * upper[t]
-                        total = total + aa[x, 4, part, :] * right
-                        total = total + aa[x, 5, part, :] * left
-                        tiles.append(total)
-                        if level + 1 < DEPTH:
-                            vv[level + 1, x + 1, f, part, :] = total
-                    fields.append(tiles)
-                return emit(level + 1, x, i, fields, carry)
-
-            carry = lax.fori_loop(0, CH, plane, (zero,) * 3)
+            columns = [[], []]
+            for m in range(NF // 2):
+                both = jnp.where(even, zr[level, 0, c, m], zr[level, 1, c, m])
+                high = both.astype(BF16)
+                low = (both - high.astype(F32)).astype(BF16)
+                columns[0].append(jnp.concatenate([high, high], 0))
+                columns[1].append(jnp.concatenate([low, low], 0))
+
+            def unit(u, nothing):
+                x0 = c * CH + u * UNIT
+                masks = []
+                for i in range(UNIT):
+                    mine = ((wide_lane >> 1) & (CH - 1)) == u * UNIT + i
+                    masks.append([jnp.where(mine, g, 0.0).astype(BF16) for g in groups])
+                left_part = []
+                for t in range(TILES):
+                    outer = [
+                        jnp.concatenate(
+                            [columns[h][m] * masks[i][t] for i in range(UNIT) for m in range(NF // 2)], 0
+                        )
+                        for h in range(2)
+                    ]
+                    left_part.append(jnp.concatenate([halves(level, x0, UNIT, t)] + outer, 1))
+                moved = jnp.dot(
+                    jnp.concatenate(left_part, 0), shift[...], preferred_element_type=F32
+                )
+                for i in range(UNIT):
+                    x = x0 + i
+                    fields = []
+                    for f in range(NF):
+                        own = tiles_of(level, x + 1, f)
+                        low = tiles_of(level, x, f)
+                        high = tiles_of(level, x + 2, f)
+                        before = jnp.broadcast_to(yr[level, 0, f, pl.ds(x, 1), :], (8, 128))
+                        after = jnp.broadcast_to(yr[level, 1, f, pl.ds(x, 1), :], (8, 128))
+                        upper, lower = shifted_rows(own, before, after, row)
+                        tiles = []
+                        for t in range(TILES):
+                            at_row = ((t * UNIT + i) * NF + f) * 8
+                            part = slice(t * 8, (t + 1) * 8)
+                            total = aa[x, 0, part, :] * high[t]
+                            total = total + aa[x, 1, part, :] * low[t]
+                            total = total + aa[x, 2, part, :] * lower[t]
+                            total = total + aa[x, 3, part, :] * upper[t]
+                            total = total + aa[x, 4, part, :] * moved[at_row:at_row + 8, 128:]
+                            total = total + aa[x, 5, part, :] * moved[at_row:at_row + 8, :128]
+                            tiles.append(total)
+                            if level + 1 < DEPTH:
+                                vv[level + 1][x + 1, f, part, :] = total
+                        fields.append(tiles)
+                    emit(level + 1, x, fields)
+                return nothing
+
+            lax.fori_loop(0, CH // UNIT, unit, 0)
             if level + 1 < DEPTH:
-                send_chunk(level + 1, q, c, carry)
+                send_chunk(level + 1, q, c)
             return nothing
 
         lax.fori_loop(0, chunks, chunk, 0)
 
     acc[...] = jnp.zeros_like(acc)
 
-    def products(x, nothing):
-        acc[...] += nt(hl[x].reshape(2 * ROWS, TILES * 128), hl[x, 0])
+    def products(g, nothing):
+        high, low = [
+            jnp.concatenate(
+                [
+                    jnp.concatenate([ref[g * GROUP + i, h] for ref in hl], 0)
+                    for i in range(GROUP)
+                ],
+                1,
+            )
+            for h in range(2)
+        ]
+        acc[...] += nt(jnp.concatenate([high, low], 0), high)
         return nothing
 
-    lax.fori_loop(0, nx, products, 0)
+    lax.fori_loop(0, nx // GROUP, products, 0)
 
     same = (iota((ROWS, ROWS), 0) & 7) == (iota((ROWS, ROWS), 1) & 7)
     mixed = jnp.where(same, acc[0:ROWS] + 2.0 * acc[ROWS:], 0.0)
@@ -382,18 +450,50 @@
             lax.fori_loop(0, chunks, drain, 0)
 
 
-def solve_kernel(wmat, factor, hl, q, r):
-    x = pl.program_id(0)
-    high, low = hl[x, 0], hl[x, 1]
-    weights = jnp.concatenate([wmat[0], wmat[0], wmat[1]], 1)
-    result = jnp.dot(weights, jnp.concatenate([high, low, high], 0), preferred_element_type=F32)
-    for f in range(NC):
-        for t in range(TILES):
-            q[f, 0, t * 8:(t + 1) * 8, :] = result[f * 8:(f + 1) * 8, t * 128:(t + 1) * 128]
-
-    @pl.when(x == 0)
-    def _():
-        r[...] = factor[:, 0:NC]
+def solve_kernel(wmat, factor, hl0, hl1, hl2, hl3, q, r, held, sems):
+    nx = hl0.shape[0]
+    r[...] = factor[:, 0:NC]
+
+    steps = nx // SPAN
+
+    def out_copy(g):
+        slot = lax.rem(g, SLOTS)
+        return pltpu.make_async_copy(held.at[slot], q.at[:, pl.ds(g * SPAN, SPAN)], sems.at[slot])
+
+    def planes(g, nothing):
+        @pl.when(g >= SLOTS)
+        def _():
+            out_copy(g - SLOTS).wait()
+
+        slot = lax.rem(g, SLOTS)
+        high, low = [
+            jnp.concatenate(
+                [
+                    jnp.concatenate([ref[g * SPAN + i, h] for ref in (hl0, hl1, hl2, hl3)], 0)
+                    for i in range(SPAN)
+                ],
+                1,
+            )
+            for h in range(2)
+        ]
+        result = jnp.dot(wmat[0], high, preferred_element_type=F32)
+        result = result + jnp.dot(wmat[0], low, preferred_element_type=F32)
+        result = result + jnp.dot(wmat[1], high, preferred_element_type=F32)
+        for f in range(NC):
+            for i in range(SPAN):
+                for t in range(TILES):
+                    col = (i * TILES + t) * 128
+                    held[slot, f, i, t * 8:(t + 1) * 8, :] = result[f * 8:(f + 1) * 8, col:col + 128]
+        out_copy(g).start()
+        return nothing
+
+    lax.fori_loop(0, steps, planes, 0)
+
+    def drain(g, nothing):
+        out_copy(g).wait()
+        return nothing
+
+    lax.fori_loop(max(steps - SLOTS, 0), steps, drain, 0)
 
 
 def on_device(sizes, right_sides, permeability):
@@ -403,27 +503,29 @@
     n1, n2 = sizes[0] * sizes[1], sizes[2]
     dma = pltpu.SemaphoreType.DMA
     vmem = pl.BlockSpec(memory_space=pltpu.VMEM)
-    hl, wmat, factor = pl.pallas_call(
+    *hl, wmat, factor = pl.pallas_call(
         functools.partial(basis_kernel, sizes, cells),
         out_shape=(
-            pltpu.VMEM((nx, 2, ROWS, TILES * 128), BF16),
+            *[pltpu.VMEM((nx, 2, BAND, TILES * 128), BF16)] * LEVELS,
             pltpu.VMEM((2, ROWS, ROWS), BF16),
             pltpu.VMEM((NC, 128), F32),
         ),
         in_specs=[pl.BlockSpec(memory_space=pl.ANY)] * 2,
-        out_specs=(vmem, vmem, vmem),
+        out_specs=(vmem,) * (LEVELS + 2),
         scratch_shapes=[
             pltpu.VMEM((nx + 2, ny, 128), F32),
             pltpu.VMEM((2, nx, 128), F32),
             pltpu.VMEM((2, nx, 128), F32),
             pltpu.VMEM((2, 8, 128), F32),
             pltpu.VMEM((2, 2, 8, 128), F32),
-            pltpu.VMEM((DEPTH, nx + 2, NF, ny, 128), F32),
+            *[pltpu.VMEM((nx + 2, NF, ny, 128), F32)] * DEPTH,
             pltpu.VMEM((nx, 6, ny, 128), F32),
             pltpu.VMEM((DEPTH, 2, NF, nx, 128), F32),
             pltpu.VMEM((DEPTH, 2, NF, nx, 128), F32),
             pltpu.VMEM((DEPTH, chunks, NF // 2, 8, 128), F32),
             pltpu.VMEM((DEPTH, 2, chunks, NF // 2, 8, 128), F32),
+            pltpu.VMEM((512, 256), BF16),
+            pltpu.VMEM((256, 128), BF16),
             pltpu.VMEM((2 * ROWS, ROWS), F32),
             pltpu.VMEM((2, 8, 128), F32),
             pltpu.VMEM((n1, 8, 128), F32),
@@ -443,19 +545,19 @@
     )(right_sides, permeability)
     return pl.pallas_call(
         solve_kernel,
-        grid=(nx,),
         out_shape=(
             jax.ShapeDtypeStruct((NC, nx, ny, 128), F32),
             jax.ShapeDtypeStruct((NC, NC), F32),
         ),
-        in_specs=[vmem, vmem, vmem],
-        out_specs=(
-            pl.BlockSpec((NC, 1, ny, 128), lambda x: (0, x, 0, 0)),
-            pl.BlockSpec((NC, NC), lambda x: (0, 0)),
-        ),
-        compiler_params=pltpu.CompilerParams(vmem_limit_bytes=8 * 1024 * 1024),
+        in_specs=[vmem] * (LEVELS + 2),
+        out_specs=(pl.BlockSpec(memory_space=pl.ANY), vmem),
+        scratch_shapes=[
+            pltpu.VMEM((SLOTS, NC, SPAN, ny, 128), F32),
+            dma((SLOTS,)),
+        ],
+        compiler_params=pltpu.CompilerParams(vmem_limit_bytes=12 * 1024 * 1024),
         name="solve",
-    )(wmat, factor, hl)
+    )(wmat, factor, *hl)
 
 
 def solution(mesh):

time: 100 us -> 60.6 us (0.61)
  Pallas kernels: 99.4 us -> 59.8 us
    pallas_call x1, Pallas kernels: 81.4 us -> 51.9 us  [on_device(): pl.pallas_call(functools.partial(basis_kernel, sizes, cells), out_shape=(...]
    pallas_call x1, Pallas kernels: 18 us -> 7.91 us  [on_device(): pl.pallas_call(solve_kernel, out_shape=(jax.ShapeDtypeStruct((NC, nx, ny,...]
where the time goes in v2:
time: 60.6 us; the launch traced here: 60.5 us
  Pallas kernels  59.8 us (99%)
  between operations  0.64 us (1%)
    pallas_call x1, Pallas kernels, on_device(): pl.pallas_call(functools.partial(basis_kernel, sizes, cells), out_shape=(...  51.9 us
    pallas_call x1, Pallas kernels, on_device(): pl.pallas_call(solve_kernel, out_shape=(jax.ShapeDtypeStruct((NC, nx, ny,...  7.91 us

profile of v2, /device:TPU:1, one launch (start us, length us, event | category | flops | bytes accessed | tf_op | source)
XLA Modules:
  0.0 60.5 jit_solution(5160586603162923185)
XLA Ops:
  0.6 51.9 %basis.1 = (bf16[32,2,48,512]{3,2,1,0:T(8,128)(2,1)S(1)}, bf16[32,2,48,512]{3,2,1,0:T(8,128)(2,1)S(1)}, bf16[32,2,48,512]{3,2,1,0:T(8,128)(2,1)S(1)}, bf16[32,2,...) custom-call(f32[6,32,32,128]{3,2,1,0:T(8,128)} %rs.1, f32[32,32,128]{2,1,0:T(8,128)} %kap.1), custom_call_target="tpu_custom_call" | custom-call | tf_op jit(solution)/shard_map/basis/pallas_call | solution.py:506
  52.5 7.9 %solve.1 = (f32[24,32,32,128]{3,2,1,0:T(8,128)}, f32[24,24]{1,0:T(8,128)}) custom-call(bf16[2,192,192]{2,1,0:T(8,128)(2,1)S(1)} %get-tuple-element.8.wmat, f32[24,128]{1,0:T(8,128)S(1)} %get-tuple-element.9.factor, bf16[32,2,48,512]{3,2,1,0:T(8,128)(2,1)S(1)} %get-tuple-element.10.hl0, bf16[32,2,48,512]{3,2,1,0:T(8,128)(2,1)S(1)} %get-tuple-element.11.hl1, ...), custom_call_target="tpu_custom_call" | custom-call | tf_op jit(solution)/shard_map/solve/pallas_call | solution.py:546

commit v3 on v2

--- a/solution.py
+++ b/solution.py
@@ -60,14 +60,14 @@
 
 def basis_kernel(
     sizes, cells, rs, kap, hl0, hl1, hl2, hl3, wmat, factor,
-    kp, kys, kyr, kzs, kzr, v0, v1, v2, aa, ys, yr, zs, zr, shift, gather, acc, msg, slot1, slot2,
+    kp, kys, kyr, kzs, kzr, v0, v1, v2, aa, ys, yr, zs, zr, shift, gather, acc, msg, slot,
     load_sem, ks_sem, kr_sem, xs_sem, xr_sem, ys_sem, yr_sem, zs_sem, zr_sem,
-    s1_sem, r1_sem, s2_sem, r2_sem,
+    s_sem, r_sem,
 ):
     hl = (hl0, hl1, hl2, hl3)
     vv = (v0, v1, v2)
     gx, gy, gz = sizes
-    nx = kp.shape[0] - 2
+    nx, ny = kp.shape[0] - 2, kp.shape[1]
     chunks = nx // CH
     ix, iy, iz = lax.axis_index("gx"), lax.axis_index("gy"), lax.axis_index("gz")
     at = {"gx": ix, "gy": iy, "gz": iz}
@@ -80,19 +80,19 @@
     kap_copy.start()
     field_copies = []
     for f in range(NF):
-        copy = pltpu.make_async_copy(rs.at[f], v0.at[pl.ds(1, nx), f], load_sem.at[f])
+        copy = pltpu.make_async_copy(rs.at[f], v0.at[pl.ds(1, nx), f, pl.ds(8, ny)], load_sem.at[f])
         copy.start()
         field_copies.append(copy)
 
     n1 = gx * gy
     rank1 = ix * gy + iy
-    group1 = []
+    barrier = pltpu.get_barrier_semaphore()
+    greeted = []
     for d in range(1, n1):
         other = lax.rem(rank1 + d, n1)
-        group1.append({"gx": other // gy, "gy": lax.rem(other, gy)})
-    group2 = [{"gz": lax.rem(iz + d, gz)} for d in range(1, gz)]
-    barrier = pltpu.get_barrier_semaphore()
-    for device in group1 + group2:
+        greeted.append({"gx": other // gy, "gy": lax.rem(other, gy)})
+    greeted += [{"gz": lax.rem(iz + d, gz)} for d in range(1, gz)]
+    for device in greeted:
         pl.semaphore_signal(barrier, inc=1, device_id=device, device_id_type=MESH)
 
     lane = iota((8, 128), 1)
@@ -131,7 +131,7 @@
     packed = lax.fori_loop(0, nx, pack_kap, (zero, zero), unroll=8)
     for m in range(2):
         kzs[m] = packed[m]
-    pl.semaphore_wait(barrier, n1 - 1 + gz - 1)
+    pl.semaphore_wait(barrier, n1 + gz - 2)
 
     kap_sends = [
         remote(kp.at[nx], kp.at[0], ks_sem.at[0], kr_sem.at[0], toward("gx", 1)),
@@ -147,7 +147,7 @@
     def x_copy(level, side):
         src, dst = (nx, 0) if side == 0 else (1, nx + 1)
         return remote(
-            vv[level].at[src], vv[level].at[dst], xs_sem.at[level, side], xr_sem.at[level, side],
+            vv[level].at[src, :, pl.ds(8, ny)], vv[level].at[dst, :, pl.ds(8, ny)], xs_sem.at[level, side], xr_sem.at[level, side],
             toward("gx", 1 - 2 * side),
         )
 
@@ -213,8 +213,8 @@
         for side in range(2):
             z_copy(level, side, c).start()
 
-    def tiles_of(level, plane, f):
-        return [vv[level][plane, f, t * 8:(t + 1) * 8, :] for t in range(TILES)]
+    def tiles_of(level, plane, f, by=0):
+        return [vv[level][plane, f, pl.ds(8 + by + t * 8, 8), :] for t in range(TILES)]
 
     def order(q):
         return lax.rem(q * (chunks - 1), chunks)
@@ -294,6 +294,14 @@
             def _():
                 x_copy(level, 1).wait_recv()
 
+            def outer_rows(i, nothing):
+                x = c * CH + i
+                for f in range(NF):
+                    vv[level][x + 1, f, 7:8, :] = yr[level, 0, f, pl.ds(x, 1), :]
+                    vv[level][x + 1, f, ny + 8:ny + 9, :] = yr[level, 1, f, pl.ds(x, 1), :]
+                return nothing
+
+            lax.fori_loop(0, CH, outer_rows, 0, unroll=4)
             columns = [[], []]
             for m in range(NF // 2):
                 both = jnp.where(even, zr[level, 0, c, m], zr[level, 1, c, m])
@@ -324,12 +332,10 @@
                     x = x0 + i
                     fields = []
                     for f in range(NF):
-                        own = tiles_of(level, x + 1, f)
                         low = tiles_of(level, x, f)
                         high = tiles_of(level, x + 2, f)
-                        before = jnp.broadcast_to(yr[level, 0, f, pl.ds(x, 1), :], (8, 128))
-                        after = jnp.broadcast_to(yr[level, 1, f, pl.ds(x, 1), :], (8, 128))
-                        upper, lower = shifted_rows(own, before, after, row)
+                        upper = tiles_of(level, x + 1, f, -1)
+                        lower = tiles_of(level, x + 1, f, 1)
                         tiles = []
                         for t in range(TILES):
                             at_row = ((t * UNIT + i) * NF + f) * 8
@@ -342,7 +348,7 @@
                             total = total + aa[x, 5, part, :] * moved[at_row:at_row + 8, :128]
                             tiles.append(total)
                             if level + 1 < DEPTH:
-                                vv[level + 1][x + 1, f, part, :] = total
+                                vv[level + 1][x + 1, f, 8 + t * 8:16 + t * 8, :] = total
                         fields.append(tiles)
                     emit(level + 1, x, fields)
                 return nothing
@@ -380,32 +386,31 @@
     small = jnp.dot(small, spread, precision=HIGH, preferred_element_type=F32)
     message = small[0:8] + lane_roll(small[8:16], 32) + lane_roll(small[16:24], 64)
 
-    msg[0] = message
-    slot1[rank1] = message
-    sends1 = []
-    for d, device in enumerate(group1):
-        copy = remote(msg.at[0], slot1.at[rank1], s1_sem.at[d], r1_sem.at[rank1], device)
-        copy.start()
-        sends1.append(copy)
-    for d in range(1, n1):
-        source = lax.rem(rank1 + d, n1)
-        remote(msg.at[0], slot1.at[source], s1_sem.at[0], r1_sem.at[source], group1[0]).wait_recv()
-    message = slot1[0]
-    for d in range(1, n1):
-        message = message + slot1[d]
-    msg[1] = message
-    slot2[iz] = message
-    sends2 = []
-    for d, device in enumerate(group2):
-        copy = remote(msg.at[1], slot2.at[iz], s2_sem.at[d], r2_sem.at[iz], device)
-        copy.start()
-        sends2.append(copy)
-    for d in range(1, gz):
-        source = lax.rem(iz + d, gz)
-        remote(msg.at[1], slot2.at[source], s2_sem.at[0], r2_sem.at[source], group2[0]).wait_recv()
-    message = slot2[0]
-    for d in range(1, gz):
-        message = message + slot2[d]
+    sum_sends = []
+    for number, count in enumerate((gx * gy, gz)):
+        rank = ix * gy + iy if number == 0 else iz
+        send, receive, slots = s_sem.at[number], r_sem.at[number], slot.at[number]
+
+        def member(d):
+            other = lax.rem(rank + d, count)
+            if number:
+                return other, {"gz": other}
+            return other, {"gx": other // gy, "gy": lax.rem(other, gy)}
+
+        msg[number] = message
+        slots[rank] = message
+        for d in range(1, count):
+            copy = remote(
+                msg.at[number], slots.at[rank], send.at[d], receive.at[rank], member(d)[1]
+            )
+            copy.start()
+            sum_sends.append(copy)
+        for d in range(1, count):
+            source, device = member(d)
+            remote(msg.at[number], slots.at[source], send.at[d], receive.at[source], device).wait_recv()
+        message = slots[0]
+        for d in range(1, count):
+            message = message + slots[d]
 
     message = message * (0.5 / cells)
     lanes = iota((NC, 128), 1)
@@ -416,13 +421,22 @@
     padded = jnp.concatenate([half, jnp.zeros((128 - NC, 128), F32)], 0)
     matrix = half + nt(identity, padded, HIGH) + (lanes == rows + 32).astype(F32)
     pivots = jnp.ones((NC, 128), F32)
-    for k in range(NC):
-        pivot_row = jnp.broadcast_to(matrix[k:k + 1, :], (NC, 128))
-        column = jnp.broadcast_to(matrix[:, k:k + 1], (NC, 128))
-        pivot = jnp.broadcast_to(column[k:k + 1, :], (NC, 128))
-        pivots = jnp.where(rows == k, pivot, pivots)
-        factors = jnp.where(rows > k, column / pivot, 0.0)
-        matrix = matrix - factors * pivot_row
+
+    def across(value, k):
+        return jnp.broadcast_to(value[k:k + 1, :], (NC, 128))
+
+    for first in range(0, NC, NF):
+        columns = [
+            jnp.broadcast_to(matrix[:, k:k + 1], (NC, 128)) for k in range(first, first + NF)
+        ]
+        for j in range(NF):
+            k = first + j
+            pivot = across(columns[j], k)
+            pivots = jnp.where(rows == k, pivot, pivots)
+            factors = jnp.where(rows > k, columns[j] * reciprocal(pivot), 0.0)
+            for later in range(j + 1, NF):
+                columns[later] = columns[later] - factors * across(columns[j], first + later)
+            matrix = matrix - factors * across(matrix, k)
     matrix = matrix * (1.0 / jnp.sqrt(pivots))
     factor[...] = jnp.where((lanes >= rows) & (lanes < NC), matrix, 0.0)
     inverse = jnp.where(lanes <= rows, lane_roll(matrix, 96), 0.0)
@@ -436,7 +450,7 @@
         wide = jnp.where(same, nt(wide, spread), 0.0).astype(BF16)
         wmat[which] = wide
 
-    for copy in kap_sends + sends1 + sends2:
+    for copy in kap_sends + sum_sends:
         copy.wait_send()
     for level in range(DEPTH):
         for side in range(2):
@@ -500,7 +514,7 @@
     nx, ny, nz = permeability.shape
     chunks = nx // CH
     cells = float(nx * ny * nz * sizes[0] * sizes[1] * sizes[2])
-    n1, n2 = sizes[0] * sizes[1], sizes[2]
+    most = max(sizes[0] * sizes[1], sizes[2])
     dma = pltpu.SemaphoreType.DMA
     vmem = pl.BlockSpec(memory_space=pltpu.VMEM)
     *hl, wmat, factor = pl.pallas_call(
@@ -518,7 +532,7 @@
             pltpu.VMEM((2, nx, 128), F32),
             pltpu.VMEM((2, 8, 128), F32),
             pltpu.VMEM((2, 2, 8, 128), F32),
-            *[pltpu.VMEM((nx + 2, NF, ny, 128), F32)] * DEPTH,
+            *[pltpu.VMEM((nx + 2, NF, ny + 16, 128), F32)] * DEPTH,
             pltpu.VMEM((nx, 6, ny, 128), F32),
             pltpu.VMEM((DEPTH, 2, NF, nx, 128), F32),
             pltpu.VMEM((DEPTH, 2, NF, nx, 128), F32),
@@ -528,15 +542,13 @@
             pltpu.VMEM((256, 128), BF16),
             pltpu.VMEM((2 * ROWS, ROWS), F32),
             pltpu.VMEM((2, 8, 128), F32),
-            pltpu.VMEM((n1, 8, 128), F32),
-            pltpu.VMEM((n2, 8, 128), F32),
+            pltpu.VMEM((2, most, 8, 128), F32),
             dma((NF + 1,)),
             dma((6,)), dma((6,)),
             dma((DEPTH, 2)), dma((DEPTH, 2)),
             dma((DEPTH, 2, chunks)), dma((DEPTH, 2, chunks)),
             dma((DEPTH, 2, chunks)), dma((DEPTH, 2, chunks)),
-            dma((n1 - 1,)), dma((n1,)),
-            dma((n2 - 1,)), dma((n2,)),
+            dma((2, most)), dma((2, most)),
         ],
         compiler_params=pltpu.CompilerParams(
             collective_id=0, has_side_effects=True, vmem_limit_bytes=44 * 1024 * 1024

time: 60.6 us -> 58.3 us (0.962)
  Pallas kernels: 59.8 us -> 57.6 us
    pallas_call x1, Pallas kernels: 51.9 us -> 49.6 us  [on_device(): pl.pallas_call(functools.partial(basis_kernel, sizes, cells), out_shape=(...]
where the time goes in v3:
time: 58.3 us; the launch traced here: 58.2 us
  Pallas kernels  57.6 us (99%)
  between operations  0.64 us (1%)
    pallas_call x1, Pallas kernels, on_device(): pl.pallas_call(functools.partial(basis_kernel, sizes, cells), out_shape=(...  49.6 us
    pallas_call x1, Pallas kernels, on_device(): pl.pallas_call(solve_kernel, out_shape=(jax.ShapeDtypeStruct((NC, nx, ny,...  7.91 us

profile of v3, /device:TPU:1, one launch (start us, length us, event | category | flops | bytes accessed | tf_op | source)
XLA Modules:
  0.0 58.2 jit_solution(1773100528657435091)
XLA Ops:
  0.6 49.6 %basis.1 = (bf16[32,2,48,512]{3,2,1,0:T(8,128)(2,1)S(1)}, bf16[32,2,48,512]{3,2,1,0:T(8,128)(2,1)S(1)}, bf16[32,2,48,512]{3,2,1,0:T(8,128)(2,1)S(1)}, bf16[32,2,...) custom-call(f32[6,32,32,128]{3,2,1,0:T(8,128)} %rs.1, f32[32,32,128]{2,1,0:T(8,128)} %kap.1), custom_call_target="tpu_custom_call" | custom-call | tf_op jit(solution)/shard_map/basis/pallas_call | solution.py:520
  50.3 7.9 %solve.1 = (f32[24,32,32,128]{3,2,1,0:T(8,128)}, f32[24,24]{1,0:T(8,128)}) custom-call(bf16[2,192,192]{2,1,0:T(8,128)(2,1)S(1)} %get-tuple-element.8.wmat, f32[24,128]{1,0:T(8,128)S(1)} %get-tuple-element.9.factor, bf16[32,2,48,512]{3,2,1,0:T(8,128)(2,1)S(1)} %get-tuple-element.10.hl0, bf16[32,2,48,512]{3,2,1,0:T(8,128)(2,1)S(1)} %get-tuple-element.11.hl1, ...), custom_call_target="tpu_custom_call" | custom-call | tf_op jit(solution)/shard_map/solve/pallas_call | solution.py:558

commit v4 on v3

--- a/solution.py
+++ b/solution.py
@@ -273,7 +273,7 @@
                 aa[x, n, part, :] = faces[n] * scale
         return nothing
 
-    lax.fori_loop(0, nx, weights, 0, unroll=2)
+    lax.fori_loop(0, nx, weights, 0, unroll=4)
 
     wide_lane = iota((16, 128), 1)
     second = jnp.where(iota((16, 128), 0) < 8, 0, TILES)
@@ -442,13 +442,20 @@
     inverse = jnp.where(lanes <= rows, lane_roll(matrix, 96), 0.0)
 
     padded = jnp.concatenate([inverse, jnp.zeros((128 - NC, 128), F32)], 0)
-    high = padded.astype(BF16)
-    low = (padded - high.astype(F32)).astype(BF16)
-    spread = spread.astype(BF16)
-    for which, piece in enumerate((high, low)):
-        wide = jnp.dot(spread, piece, preferred_element_type=F32).astype(BF16)
-        wide = jnp.where(same, nt(wide, spread), 0.0).astype(BF16)
-        wmat[which] = wide
+    high = padded.astype(BF16).astype(F32)
+    both = (high + lane_roll((padded - high).astype(BF16).astype(F32), NC)).astype(BF16)
+    tall = jnp.dot(spread.astype(BF16), both, preferred_element_type=F32).astype(BF16)
+    place, chosen = iota((3 * ROWS, 128), 0), iota((3 * ROWS, 128), 1)
+    kind = (place >= 3 * BAND).astype(jnp.int32)
+    for level in range(2, LEVELS):
+        kind = kind + (place >= 3 * BAND * level).astype(jnp.int32)
+    inner = place - 3 * BAND * kind
+    place = kind * BAND + jnp.where(
+        inner < BAND, inner, jnp.where(inner < 2 * BAND, inner - BAND, inner - 2 * BAND + ROWS)
+    )
+    wide = nt(tall, ((place >> 3) == chosen).astype(F32).astype(BF16))
+    same = (iota((ROWS, 3 * ROWS), 0) & 7) == (iota((ROWS, 3 * ROWS), 1) & 7)
+    wmat[...] = jnp.where(same, wide, 0.0).astype(BF16)
 
     for copy in kap_sends + sum_sends:
         copy.wait_send()
@@ -480,19 +487,23 @@
             out_copy(g - SLOTS).wait()
 
         slot = lax.rem(g, SLOTS)
-        high, low = [
-            jnp.concatenate(
-                [
-                    jnp.concatenate([ref[g * SPAN + i, h] for ref in (hl0, hl1, hl2, hl3)], 0)
-                    for i in range(SPAN)
-                ],
-                1,
+        data = []
+        for ref in (hl0, hl1, hl2, hl3):
+            high, low = [
+                jnp.concatenate([ref[g * SPAN + i, h] for i in range(SPAN)], 1) for h in range(2)
+            ]
+            data += [high, low, high]
+        data = jnp.concatenate(data, 0)
+        result = None
+        for start in range(0, 3 * ROWS, 256):
+            stop = min(start + 256, 3 * ROWS)
+            above = start // (3 * BAND) * BAND
+            part = jnp.dot(
+                wmat[above:, start:stop], data[start:stop], preferred_element_type=F32
             )
-            for h in range(2)
-        ]
-        result = jnp.dot(wmat[0], high, preferred_element_type=F32)
-        result = result + jnp.dot(wmat[0], low, preferred_element_type=F32)
-        result = result + jnp.dot(wmat[1], high, preferred_element_type=F32)
+            if result is not None:
+                part = jnp.concatenate([result[:above], result[above:] + part], 0)
+            result = part
         for f in range(NC):
             for i in range(SPAN):
                 for t in range(TILES):
@@ -521,7 +532,7 @@
         functools.partial(basis_kernel, sizes, cells),
         out_shape=(
             *[pltpu.VMEM((nx, 2, BAND, TILES * 128), BF16)] * LEVELS,
-            pltpu.VMEM((2, ROWS, ROWS), BF16),
+            pltpu.VMEM((ROWS, 3 * ROWS), BF16),
             pltpu.VMEM((NC, 128), F32),
         ),
         in_specs=[pl.BlockSpec(memory_space=pl.ANY)] * 2,

time: 58.3 us -> 55.2 us (0.947)
  Pallas kernels: 57.6 us -> 54.4 us
    pallas_call x1, Pallas kernels: 49.6 us -> 48 us  [on_device(): pl.pallas_call(functools.partial(basis_kernel, sizes, cells), out_shape=(...]
    pallas_call x1, Pallas kernels: 7.91 us -> 6.43 us  [on_device(): pl.pallas_call(solve_kernel, out_shape=(jax.ShapeDtypeStruct((NC, nx, ny,...]
where the time goes in v4:
time: 55.2 us; the launch traced here: 55.1 us
  Pallas kernels  54.4 us (99%)
  between operations  0.64 us (1%)
    pallas_call x1, Pallas kernels, on_device(): pl.pallas_call(functools.partial(basis_kernel, sizes, cells), out_shape=(...  48 us
    pallas_call x1, Pallas kernels, on_device(): pl.pallas_call(solve_kernel, out_shape=(jax.ShapeDtypeStruct((NC, nx, ny,...  6.43 us

profile of v4, /device:TPU:1, one launch (start us, length us, event | category | flops | bytes accessed | tf_op | source)
XLA Modules:
  0.0 55.1 jit_solution(723974032083812641)
XLA Ops:
  0.6 48.0 %basis.1 = (bf16[32,2,48,512]{3,2,1,0:T(8,128)(2,1)S(1)}, bf16[32,2,48,512]{3,2,1,0:T(8,128)(2,1)S(1)}, bf16[32,2,48,512]{3,2,1,0:T(8,128)(2,1)S(1)}, bf16[32,2,...) custom-call(f32[6,32,32,128]{3,2,1,0:T(8,128)} %rs.1, f32[32,32,128]{2,1,0:T(8,128)} %kap.1), custom_call_target="tpu_custom_call" | custom-call | tf_op jit(solution)/shard_map/basis/pallas_call | solution.py:531
  48.7 6.4 %solve.1 = (f32[24,32,32,128]{3,2,1,0:T(8,128)}, f32[24,24]{1,0:T(8,128)}) custom-call(bf16[192,576]{1,0:T(8,128)(2,1)S(1)} %get-tuple-element.8.wmat, f32[24,128]{1,0:T(8,128)S(1)} %get-tuple-element.9.factor, bf16[32,2,48,512]{3,2,1,0:T(8,128)(2,1)S(1)} %get-tuple-element.10.hl0, bf16[32,2,48,512]{3,2,1,0:T(8,128)(2,1)S(1)} %get-tuple-element.11.hl1, ...), custom_call_target="tpu_custom_call" | custom-call | tf_op jit(solution)/shard_map/solve/pallas_call | solution.py:569

commit v5 on v4

--- a/solution.py
+++ b/solution.py
@@ -204,10 +204,6 @@
             @pl.when(q == 0)
             def _():
                 x_copy(level, 1).start()
-
-            @pl.when(q == 1)
-            def _():
-                x_copy(level, 0).start()
 
         pack_chunk(level, c)
         for side in range(2):
@@ -286,10 +282,6 @@
                 y_copy(level, side, c).wait_recv()
                 z_copy(level, side, c).wait_recv()
 
-            @pl.when(q == 0)
-            def _():
-                x_copy(level, 0).wait_recv()
-
             @pl.when(q == 1)
             def _():
                 x_copy(level, 1).wait_recv()
@@ -311,10 +303,16 @@
                 columns[1].append(jnp.concatenate([low, low], 0))
 
             def unit(u, nothing):
-                x0 = c * CH + u * UNIT
+                first = (CH // UNIT - 1 - u) * UNIT
+                x0 = c * CH + first
+
+                @pl.when((q == 0) & (u == CH // UNIT - 1))
+                def _():
+                    x_copy(level, 0).wait_recv()
+
                 masks = []
                 for i in range(UNIT):
-                    mine = ((wide_lane >> 1) & (CH - 1)) == u * UNIT + i
+                    mine = ((wide_lane >> 1) & (CH - 1)) == first + i
                     masks.append([jnp.where(mine, g, 0.0).astype(BF16) for g in groups])
                 left_part = []
                 for t in range(TILES):
@@ -351,6 +349,11 @@
                                 vv[level + 1][x + 1, f, 8 + t * 8:16 + t * 8, :] = total
                         fields.append(tiles)
                     emit(level + 1, x, fields)
+                if level + 1 < DEPTH:
+                    @pl.when((q == 1) & (u == 0))
+                    def _():
+                        x_copy(level + 1, 0).start()
+
                 return nothing
 
             lax.fori_loop(0, CH // UNIT, unit, 0)
@@ -405,6 +408,19 @@
             )
             copy.start()
             sum_sends.append(copy)
+        if number == 0:
+            for copy in kap_sends:
+                copy.wait_send()
+            for level in range(DEPTH):
+                for side in range(2):
+                    x_copy(level, side).wait_send()
+
+                    def drain(c, nothing, level=level, side=side):
+                        y_copy(level, side, c).wait_send()
+                        z_copy(level, side, c).wait_send()
+                        return nothing
+
+                    lax.fori_loop(0, chunks, drain, 0)
         for d in range(1, count):
             source, device = member(d)
             remote(msg.at[number], slots.at[source], send.at[d], receive.at[source], device).wait_recv()
@@ -457,18 +473,8 @@
     same = (iota((ROWS, 3 * ROWS), 0) & 7) == (iota((ROWS, 3 * ROWS), 1) & 7)
     wmat[...] = jnp.where(same, wide, 0.0).astype(BF16)
 
-    for copy in kap_sends + sum_sends:
+    for copy in sum_sends:
         copy.wait_send()
-    for level in range(DEPTH):
-        for side in range(2):
-            x_copy(level, side).wait_send()
-
-            def drain(c, nothing, level=level, side=side):
-                y_copy(level, side, c).wait_send()
-                z_copy(level, side, c).wait_send()
-                return nothing
-
-            lax.fori_loop(0, chunks, drain, 0)
 
 
 def solve_kernel(wmat, factor, hl0, hl1, hl2, hl3, q, r, held, sems):

time: 55.2 us -> 55.1 us (level)
  no operation moved by 1% of the time
where the time goes in v5:
time: 55.1 us; the launch traced here: 55 us
  Pallas kernels  54.4 us (99%)
  between operations  0.64 us (1%)
    pallas_call x1, Pallas kernels, on_device(): pl.pallas_call(functools.partial(basis_kernel, sizes, cells), out_shape=(...  47.9 us
    pallas_call x1, Pallas kernels, on_device(): pl.pallas_call(solve_kernel, out_shape=(jax.ShapeDtypeStruct((NC, nx, ny,...  6.43 us

profile of v5, /device:TPU:1, one launch (start us, length us, event | category | flops | bytes accessed | tf_op | source)
XLA Modules:
  0.0 55.0 jit_solution(9126700040117463333)
XLA Ops:
  0.6 47.9 %basis.1 = (bf16[32,2,48,512]{3,2,1,0:T(8,128)(2,1)S(1)}, bf16[32,2,48,512]{3,2,1,0:T(8,128)(2,1)S(1)}, bf16[32,2,48,512]{3,2,1,0:T(8,128)(2,1)S(1)}, bf16[32,2,...) custom-call(f32[6,32,32,128]{3,2,1,0:T(8,128)} %rs.1, f32[32,32,128]{2,1,0:T(8,128)} %kap.1), custom_call_target="tpu_custom_call" | custom-call | tf_op jit(solution)/shard_map/basis/pallas_call | solution.py:537
  48.6 6.4 %solve.1 = (f32[24,32,32,128]{3,2,1,0:T(8,128)}, f32[24,24]{1,0:T(8,128)}) custom-call(bf16[192,576]{1,0:T(8,128)(2,1)S(1)} %get-tuple-element.8.wmat, f32[24,128]{1,0:T(8,128)S(1)} %get-tuple-element.9.factor, bf16[32,2,48,512]{3,2,1,0:T(8,128)(2,1)S(1)} %get-tuple-element.10.hl0, bf16[32,2,48,512]{3,2,1,0:T(8,128)(2,1)S(1)} %get-tuple-element.11.hl1, ...), custom_call_target="tpu_custom_call" | custom-call | tf_op jit(solution)/shard_map/solve/pallas_call | solution.py:575

commit v6 on v5

--- a/solution.py
+++ b/solution.py
@@ -228,7 +228,7 @@
             emit(0, x, [tiles_of(0, x + 1, f) for f in range(NF)])
             return nothing
 
-        lax.fori_loop(0, CH, plane, 0, unroll=2)
+        lax.fori_loop(0, CH, plane, 0, unroll=4)
         send_chunk(0, q, c)
         return nothing
 
@@ -269,7 +269,7 @@
                 aa[x, n, part, :] = faces[n] * scale
         return nothing
 
-    lax.fori_loop(0, nx, weights, 0, unroll=4)
+    lax.fori_loop(0, nx, weights, 0, unroll=8)
 
     wide_lane = iota((16, 128), 1)
     second = jnp.where(iota((16, 128), 0) < 8, 0, TILES)

time: 55.1 us -> 54.6 us (level)
  Pallas kernels: 54.4 us -> 53.8 us
where the time goes in v6:
time: 54.6 us; the launch traced here: 54.5 us
  Pallas kernels  53.8 us (99%)
  between operations  0.64 us (1%)
    pallas_call x1, Pallas kernels, on_device(): pl.pallas_call(functools.partial(basis_kernel, sizes, cells), out_shape=(...  47.4 us
    pallas_call x1, Pallas kernels, on_device(): pl.pallas_call(solve_kernel, out_shape=(jax.ShapeDtypeStruct((NC, nx, ny,...  6.43 us

profile of v6, /device:TPU:1, one launch (start us, length us, event | category | flops | bytes accessed | tf_op | source)
XLA Modules:
  0.0 54.5 jit_solution(6687653099903350863)
XLA Ops:
  0.6 47.4 %basis.1 = (bf16[32,2,48,512]{3,2,1,0:T(8,128)(2,1)S(1)}, bf16[32,2,48,512]{3,2,1,0:T(8,128)(2,1)S(1)}, bf16[32,2,48,512]{3,2,1,0:T(8,128)(2,1)S(1)}, bf16[32,2,...) custom-call(f32[6,32,32,128]{3,2,1,0:T(8,128)} %rs.1, f32[32,32,128]{2,1,0:T(8,128)} %kap.1), custom_call_target="tpu_custom_call" | custom-call | tf_op jit(solution)/shard_map/basis/pallas_call | solution.py:537
  48.0 6.4 %solve.1 = (f32[24,32,32,128]{3,2,1,0:T(8,128)}, f32[24,24]{1,0:T(8,128)}) custom-call(bf16[192,576]{1,0:T(8,128)(2,1)S(1)} %get-tuple-element.8.wmat, f32[24,128]{1,0:T(8,128)S(1)} %get-tuple-element.9.factor, bf16[32,2,48,512]{3,2,1,0:T(8,128)(2,1)S(1)} %get-tuple-element.10.hl0, bf16[32,2,48,512]{3,2,1,0:T(8,128)(2,1)S(1)} %get-tuple-element.11.hl1, ...), custom_call_target="tpu_custom_call" | custom-call | tf_op jit(solution)/shard_map/solve/pallas_call | solution.py:575
